TPU v7x, 32 devices: a whole 2x2x4 slice. The times are simulated.
32 devices in a mesh: dp: 8 (over z, x), mp: 4 (over y, core).
Axes of the slice: x: 2, y: 2, z: 4, core: 2. Of those that a mesh axis runs over, the one named last changes fastest.
Arguments:
- tokens: bfloat16 [8192, 768], P('dp'), may hold values from -6 to 6
- lengths: int32 [16, 7], P('dp'), may hold values from 1 to 128, 512 in all within a row
- send_slot: int32 [96], P('dp'), may hold values from 0 to 15, as said below
- recv_place: int32 [128], P('dp'), may hold values from 0 to 12, as said below
- w_query: bfloat16 [768, 768], P(None, 'mp'), may hold values from -0.21875 to 0.21875
- b_query: float32 [768], P('mp'), may hold values from -3 to 3
- w_key: bfloat16 [768, 768], P(None, 'mp'), may hold values from -0.21875 to 0.21875
- w_value: bfloat16 [768, 768], P(None, 'mp'), may hold values from -0.21875 to 0.21875
- b_value: float32 [768], P('mp'), may hold values from -3 to 3
- w_out: bfloat16 [768, 768], P('mp'), may hold values from -1.25 to 1.25
- output_bias: float32 [768], replicated, may hold values from -3 to 3
- first_norm_gain: float32 [768], replicated, may hold values from 0.5 to 1.5
- first_norm_bias: float32 [768], replicated, may hold values from -1.75 to 1.75
- w_up: bfloat16 [768, 3072], P(None, 'mp'), may hold values from -0.21875 to 0.21875
- b_up: float32 [3072], P('mp'), may hold values from -3 to 3
- w_down: bfloat16 [3072, 768], P('mp'), may hold values from -0.109375 to 0.109375
- down_bias: float32 [768], replicated, may hold values from -3 to 3
- second_norm_gain: float32 [768], replicated, may hold values from 0.5 to 1.5
- second_norm_bias: float32 [768], replicated, may hold values from -0.3125 to 0.3125
- out_grad: bfloat16 [8192, 768], P('dp'), may hold values from -6 to 6
Outputs:
- result: bfloat16 [8192, 768], P('dp')
- pair_loss: float32 [48], P('dp')
- tokens_grad: float32 [8192, 768], P('dp')
- g_w_query: float32 [768, 768], P(None, 'mp')
- g_b_query: float32 [768], P('mp')
- g_w_key: float32 [768, 768], P(None, 'mp')
- g_w_value: float32 [768, 768], P(None, 'mp')
- g_b_value: float32 [768], P('mp')
- g_w_out: float32 [768, 768], P('mp')
- g_b_out: float32 [768], replicated
- first_gain_gradient: float32 [768], replicated
- g_bias_one: float32 [768], replicated
- g_w_up: float32 [768, 3072], P(None, 'mp')
- g_b_up: float32 [3072], P('mp')
- g_w_down: float32 [3072, 768], P('mp')
- g_b_down: float32 [768], replicated
- second_gain_gradient: float32 [768], replicated
- g_bias_two: float32 [768], replicated
Inputs may be any that keep to these rules, and one draw needn't show every extreme that they name: `send_slot`: on each dp index the 12 entries are distinct send slots; slot // 2 is the dp index that receives the sentence; at most 2 sentences go from one index to another, and each index sends exactly 2 to some peer. `recv_place`: entry i * 2 + k of a dp index's block is the place, in that index's pair order, of the sentence that dp index i puts in send slot (this index) * 2 + k, as send_slot gives; each place 0 to 11 occurs once on every index, and slots that no sentence fills hold 12.
All inputs are finite; a program needn't handle non-finite values.
Results may differ from a plain program's by a relative error of at most 0.024.
Values may be sent and summed in bfloat16 or wider, within the bound.
A program may use at most 128 MiB of HBM per device.

v0:
```python
from functools import partial

import jax
import jax.numpy as jnp
from jax import lax
from jax.sharding import PartitionSpec as P

HEAD_DIM = 64


NEG_FILL = -1e30
NORM_EPS = 1e-12
UNIT_EPS = 1e-06
SIM_SCALE = 50.0
HIGHEST = lax.Precision.HIGHEST


def times_t(left, right):
    return lax.dot_general(
        left, right, (((1,), (1,)), ((), ())), preferred_element_type=jnp.float32
    )


def t_times(left, right):
    return lax.dot_general(
        left, right, (((0,), (0,)), ((), ())), preferred_element_type=jnp.float32
    )


def standardize_rows(hidden_state):
    middle = jnp.mean(hidden_state, axis=-1, keepdims=True)
    centered = hidden_state - middle
    spread = jnp.mean(centered * centered, axis=-1, keepdims=True)
    inverse_deviation = lax.rsqrt(spread + NORM_EPS)
    return (centered * inverse_deviation, inverse_deviation[:, 0])


def norm_backward(upstream_gradient, normalized_rows, inverse_deviation, norm_gain):
    scaled_rows = upstream_gradient * norm_gain
    mean_value = jnp.mean(scaled_rows, axis=-1, keepdims=True)
    inner_product = jnp.mean(scaled_rows * normalized_rows, axis=-1, keepdims=True)
    return inverse_deviation[:, None] * (scaled_rows - mean_value - normalized_rows * inner_product)


def segment_tables(lengths, seq_len):
    ends = jnp.cumsum(lengths, axis=1)
    starts = ends - lengths
    position = jnp.arange(seq_len, dtype=jnp.int32)
    member = (position[None, None, :] >= starts[:, :, None]) & (
        position[None, None, :] < ends[:, :, None]
    )
    seg_id = jnp.sum((position[None, None, :] >= ends[:, :, None]).astype(jnp.int32), axis=1)
    return (member, seg_id)


def score_pairs(ordered):
    anchors = ordered[:, 0, :]
    positives = ordered[:, 1, :]
    anchor_unit = anchors * lax.rsqrt(jnp.sum(anchors * anchors, axis=-1, keepdims=True) + UNIT_EPS)
    positive_unit = positives * lax.rsqrt(
        jnp.sum(positives * positives, axis=-1, keepdims=True) + UNIT_EPS
    )
    logits = SIM_SCALE * lax.dot_general(
        anchor_unit,
        positive_unit,
        (((1,), (1,)), ((), ())),
        precision=HIGHEST,
        preferred_element_type=jnp.float32,
    )
    peak = jnp.max(logits, axis=-1, keepdims=True)
    log_total = peak[:, 0] + jnp.log(jnp.sum(jnp.exp(logits - peak), axis=-1))
    return log_total - jnp.diagonal(logits)


def row_attend(items):
    query_row, key_row, value_row, same_row = items
    scale = query_row.shape[-1] ** (-0.5)
    raw_scores = jnp.einsum("qhd,khd->hqk", query_row, key_row, preferred_element_type=jnp.float32)
    scores = jnp.where(same_row[None], raw_scores * scale, NEG_FILL)
    peak = jnp.max(scores, axis=-1, keepdims=True)
    exponent = jnp.exp(scores - peak)
    total = jnp.sum(exponent, axis=-1, keepdims=True)
    probs = exponent / total
    context_row = jnp.einsum(
        "hqk,khd->qhd", probs.astype(jnp.bfloat16), value_row, preferred_element_type=jnp.float32
    )
    return (context_row.astype(jnp.bfloat16), peak[..., 0] + jnp.log(total[..., 0]))


def row_grad(items):
    query_row, key_row, value_row, same_row, log_total, d_context_row = items
    scale = query_row.shape[-1] ** (-0.5)
    raw_scores = jnp.einsum("qhd,khd->hqk", query_row, key_row, preferred_element_type=jnp.float32)
    scores = jnp.where(same_row[None], raw_scores * scale, NEG_FILL)
    probs = jnp.exp(scores - log_total[..., None])
    d_probs = jnp.einsum(
        "qhd,khd->hqk", d_context_row, value_row, preferred_element_type=jnp.float32
    )
    delta = jnp.sum(probs * d_probs, axis=-1, keepdims=True)
    d_scores = (probs * (d_probs - delta) * scale).astype(jnp.bfloat16)
    d_query = jnp.einsum(
        "hqk,khd->qhd", d_scores, key_row, preferred_element_type=jnp.float32
    ).astype(jnp.bfloat16)
    d_key = jnp.einsum(
        "hqk,qhd->khd", d_scores, query_row, preferred_element_type=jnp.float32
    ).astype(jnp.bfloat16)
    d_value = jnp.einsum(
        "hqk,qhd->khd",
        probs.astype(jnp.bfloat16),
        d_context_row,
        preferred_element_type=jnp.float32,
    ).astype(jnp.bfloat16)
    return (d_query, d_key, d_value)


def on_device(
    tokens,
    lengths,
    send_slot,
    recv_place,
    w_query,
    b_query,
    w_key,
    w_value,
    b_value,
    w_out,
    output_bias,
    first_norm_gain,
    first_norm_bias,
    w_up,
    b_up,
    w_down,
    down_bias,
    second_norm_gain,
    second_norm_bias,
    out_grad,
):
    row_count = lengths.shape[0]
    token_count = tokens.shape[0]
    seq_len = token_count // row_count
    model_width = tokens.shape[1]
    local_width = w_query.shape[1]
    head_count = local_width // HEAD_DIM
    shaped = (row_count, seq_len, head_count, HEAD_DIM)
    member, seg_id = segment_tables(lengths, seq_len)
    same_piece = seg_id[:, :, None] == seg_id[:, None, :]
    input_rows = tokens.astype(jnp.float32)
    query_rows = (
        (jnp.dot(tokens, w_query, preferred_element_type=jnp.float32) + b_query)
        .astype(jnp.bfloat16)
        .reshape(shaped)
    )
    key_rows = (
        jnp.dot(tokens, w_key, preferred_element_type=jnp.float32)
        .astype(jnp.bfloat16)
        .reshape(shaped)
    )
    value_rows = (
        (jnp.dot(tokens, w_value, preferred_element_type=jnp.float32) + b_value)
        .astype(jnp.bfloat16)
        .reshape(shaped)
    )
    context_rows, log_total = lax.map(row_attend, (query_rows, key_rows, value_rows, same_piece))
    context = context_rows.reshape(token_count, local_width)
    attn_part = jnp.dot(context, w_out, preferred_element_type=jnp.float32)
    attention_grand_total = lax.psum(attn_part.astype(jnp.bfloat16), "mp").astype(jnp.float32)
    first_normalized_rows, first_inverse_deviation = standardize_rows(
        input_rows + attention_grand_total + output_bias
    )
    hidden_state = first_normalized_rows * first_norm_gain + first_norm_bias
    hidden_low = hidden_state.astype(jnp.bfloat16)
    up_value = jnp.dot(hidden_low, w_up, preferred_element_type=jnp.float32) + b_up
    active = jax.nn.gelu(up_value, approximate=False).astype(jnp.bfloat16)
    ffn_part = jnp.dot(active, w_down, preferred_element_type=jnp.float32)
    feedforward_grand_total = lax.psum(ffn_part.astype(jnp.bfloat16), "mp").astype(jnp.float32)
    second_normalized_rows, second_inverse_deviation = standardize_rows(
        hidden_state + feedforward_grand_total + down_bias
    )
    result = second_normalized_rows * second_norm_gain + second_norm_bias
    chosen = member[:, :-1].astype(jnp.float32)
    sent_sizes = lengths[:, :-1].astype(jnp.float32)
    pooled = (
        jnp.einsum(
            "rpt,rtd->rpd",
            chosen,
            result.reshape(row_count, seq_len, model_width),
            precision=HIGHEST,
        )
        / sent_sizes[:, :, None]
    )
    pooled_count = pooled.shape[0] * pooled.shape[1]
    pooled_low = pooled.reshape(pooled_count, model_width).astype(jnp.bfloat16)
    slot_count = recv_place.shape[0]
    outgoing = jnp.zeros((slot_count, model_width), jnp.bfloat16).at[send_slot].set(pooled_low)
    incoming = lax.all_to_all(outgoing, "dp", split_axis=0, concat_axis=0, tiled=True)
    ordered = (
        jnp.zeros((pooled_count + 1, model_width), jnp.bfloat16)
        .at[recv_place]
        .set(incoming)[:pooled_count]
    )
    ordered_pairs = ordered.astype(jnp.float32).reshape(pooled_count // 2, 2, model_width)
    pair_loss, pair_pullback = jax.vjp(score_pairs, ordered_pairs)
    d_ordered = (
        pair_pullback(jnp.ones_like(pair_loss))[0]
        .reshape(pooled_count, model_width)
        .astype(jnp.bfloat16)
    )
    d_padded = jnp.concatenate([d_ordered, jnp.zeros((1, model_width), jnp.bfloat16)], axis=0)
    returning = d_padded[recv_place]
    arriving = lax.all_to_all(returning, "dp", split_axis=0, concat_axis=0, tiled=True)
    d_pooled = (
        arriving[send_slot].astype(jnp.float32).reshape(row_count, pooled.shape[1], model_width)
        / sent_sizes[:, :, None]
    )
    result_gradient = out_grad.astype(jnp.float32) + jnp.einsum(
        "rpt,rpd->rtd", chosen, d_pooled, precision=HIGHEST
    ).reshape(token_count, model_width)
    second_gain_gradient = jnp.sum(result_gradient * second_normalized_rows, axis=0)
    g_bias_two = jnp.sum(result_gradient, axis=0)
    second_gradient = norm_backward(
        result_gradient, second_normalized_rows, second_inverse_deviation, second_norm_gain
    )
    g_b_down = jnp.sum(second_gradient, axis=0)
    d_two_low = second_gradient.astype(jnp.bfloat16)
    g_w_down = t_times(active, d_two_low)
    d_active = times_t(d_two_low, w_down).astype(jnp.bfloat16)
    gelu_pullback = jax.vjp(partial(jax.nn.gelu, approximate=False), up_value)[1]
    d_up = gelu_pullback(d_active.astype(jnp.float32))[0].astype(jnp.bfloat16)
    g_b_up = jnp.sum(d_up.astype(jnp.float32), axis=0)
    g_w_up = t_times(hidden_low, d_up)
    hidden_gradient = second_gradient + lax.psum(
        times_t(d_up, w_up).astype(jnp.bfloat16), "mp"
    ).astype(jnp.float32)
    first_gain_gradient = jnp.sum(hidden_gradient * first_normalized_rows, axis=0)
    g_bias_one = jnp.sum(hidden_gradient, axis=0)
    first_gradient = norm_backward(
        hidden_gradient, first_normalized_rows, first_inverse_deviation, first_norm_gain
    )
    g_b_out = jnp.sum(first_gradient, axis=0)
    d_one_low = first_gradient.astype(jnp.bfloat16)
    g_w_out = t_times(context, d_one_low)
    d_context = times_t(d_one_low, w_out).astype(jnp.bfloat16)
    d_query, d_key, d_value = lax.map(
        row_grad,
        (query_rows, key_rows, value_rows, same_piece, log_total, d_context.reshape(shaped)),
    )
    d_query = d_query.reshape(token_count, local_width)
    d_key = d_key.reshape(token_count, local_width)
    d_value = d_value.reshape(token_count, local_width)
    g_b_query = jnp.sum(d_query.astype(jnp.float32), axis=0)
    g_b_value = jnp.sum(d_value.astype(jnp.float32), axis=0)
    g_w_query = t_times(tokens, d_query)
    g_w_key = t_times(tokens, d_key)
    g_w_value = t_times(tokens, d_value)
    back_tokens = times_t(d_query, w_query) + times_t(d_key, w_key) + times_t(d_value, w_value)
    tokens_grad = first_gradient + lax.psum(back_tokens.astype(jnp.bfloat16), "mp").astype(
        jnp.float32
    )
    (
        g_w_query,
        g_b_query,
        g_w_key,
        g_w_value,
        g_b_value,
        g_w_out,
        g_b_out,
        first_gain_gradient,
        g_bias_one,
        g_w_up,
        g_b_up,
        g_w_down,
        g_b_down,
        second_gain_gradient,
        g_bias_two,
    ) = (
        lax.psum(g_w_query.astype(jnp.bfloat16), "dp").astype(jnp.float32),
        lax.psum(g_b_query.astype(jnp.bfloat16), "dp").astype(jnp.float32),
        lax.psum(g_w_key.astype(jnp.bfloat16), "dp").astype(jnp.float32),
        lax.psum(g_w_value.astype(jnp.bfloat16), "dp").astype(jnp.float32),
        lax.psum(g_b_value.astype(jnp.bfloat16), "dp").astype(jnp.float32),
        lax.psum(g_w_out.astype(jnp.bfloat16), "dp").astype(jnp.float32),
        lax.psum(g_b_out.astype(jnp.bfloat16), "dp").astype(jnp.float32),
        lax.psum(first_gain_gradient.astype(jnp.bfloat16), "dp").astype(jnp.float32),
        lax.psum(g_bias_one.astype(jnp.bfloat16), "dp").astype(jnp.float32),
        lax.psum(g_w_up.astype(jnp.bfloat16), "dp").astype(jnp.float32),
        lax.psum(g_b_up.astype(jnp.bfloat16), "dp").astype(jnp.float32),
        lax.psum(g_w_down.astype(jnp.bfloat16), "dp").astype(jnp.float32),
        lax.psum(g_b_down.astype(jnp.bfloat16), "dp").astype(jnp.float32),
        lax.psum(second_gain_gradient.astype(jnp.bfloat16), "dp").astype(jnp.float32),
        lax.psum(g_bias_two.astype(jnp.bfloat16), "dp").astype(jnp.float32),
    )
    return (
        result.astype(jnp.bfloat16),
        pair_loss,
        tokens_grad,
        g_w_query,
        g_b_query,
        g_w_key,
        g_w_value,
        g_b_value,
        g_w_out,
        g_b_out,
        first_gain_gradient,
        g_bias_one,
        g_w_up,
        g_b_up,
        g_w_down,
        g_b_down,
        second_gain_gradient,
        g_bias_two,
    )


def solution(mesh):
    placed = (
        P("dp", None),
        P("dp", None),
        P("dp"),
        P("dp"),
        P(None, "mp"),
        P("mp"),
        P(None, "mp"),
        P(None, "mp"),
        P("mp"),
        P("mp", None),
        P(),
        P(),
        P(),
        P(None, "mp"),
        P("mp"),
        P("mp", None),
        P(),
        P(),
        P(),
        P("dp", None),
    )
    return jax.shard_map(
        on_device,
        mesh=mesh,
        in_specs=placed,
        out_specs=(
            P("dp", None),
            P("dp"),
            P("dp", None),
            P(None, "mp"),
            P("mp"),
            P(None, "mp"),
            P(None, "mp"),
            P("mp"),
            P("mp", None),
            P(),
            P(),
            P(),
            P(None, "mp"),
            P("mp"),
            P("mp", None),
            P(),
            P(),
            P(),
        ),
        check_vma=False,
    )
```

profile of v0, /device:TPU:0, one launch (start us, length us, event | category | flops | bytes accessed | tf_op | source)
XLA Modules:
  0.0 510.0 jit_solution(7008541518479839719)
XLA Ops:
  8.7 2.9 fusion.97
  11.7 2.0 reshape.207
  13.7 1.8 copy.55
  15.5 2.4 fusion.98
  17.9 2.0 reshape.208
  19.9 1.8 copy.56
  21.7 2.4 convolution_convert_fusion.7
  24.1 2.0 reshape.209
  26.1 1.8 copy.57
  28.7 8.8 %while.26 = (s32[]{:T(128)}, bf16[2,512,3,64]{1,3,2,0:T(8,128)(2,1)}, f32[2,3,512]{2,1,0:T(4,128)S(1)}, bf16[2,512,3,64]{1,3,2,0:T(8,128)(2,1)}, pred[2,512,512]...) while((s32[]{:T(128)}, ...), condition=%wide.region_5.6_spmd, body=%wide.region_2.5_spmd.sunk | while | flops 210860544 | bytes 13168761 | solution.py:163
  28.7 1.8 fusion.223
  31.3 1.8 fusion.225
  33.1 1.8 fusion.223
  35.7 1.8 fusion.225
  37.4 1.4 copy.58
  39.7 2.7 convolution_convert_fusion.3
  42.7 45.4 %all-reduce.11.cloned.1.call-done = bf16[1024,768]{1,0:T(8,128)(2,1)} async-done(((bf16[1024,768]{1,0:T(8,128)(2,1)}), bf16[1024,768]{1,0:T(8,128)(2,1)}) %all-reduce.11.cloned.1.call-update) | async-done | bytes 1572880 | tf_op jit(solution)/shard_map/psum | solution.py:166
  88.1 2.1 fusion.96
  91.2 9.8 %multiply_convert_fusion.1 = (bf16[1024,768]{1,0:T(8,128)(2,1)S(1)}, f32[1024,768]{1,0:T(8,128)}, f32[1024,768]{1,0:T(8,128)}) fusion(f32[768]{0:T(1024)S(1)} %copy-done.42, bf16[768,768]{1,0:T(8,128)(2,1)S(1)} %copy-done, f32[768]{0:T(1024)S(1)} %copy-done.38, f32[768]{0:T(1024)S(1)} %copy-done.32, f32[1024]{0:T(1024)S(1)} %add_rsqrt_fusion.1, ...), kind=kOutput, calls=%fused_computation.98 | convolution fusion | flops 1266941952 | bytes 12210176 | tf_op jit(solution)/shard_map/dot_general | solution.py:172
  101.0 1.2 copy-done.48
  102.3 2.5 convolution_convert_fusion.2
  105.0 43.0 %all-reduce.13.cloned.1.call-done = bf16[1024,768]{1,0:T(8,128)(2,1)} async-done(((bf16[1024,768]{1,0:T(8,128)(2,1)}), bf16[1024,768]{1,0:T(8,128)(2,1)}) %all-reduce.13.cloned.1.call-update) | async-done | bytes 1572880 | tf_op jit(solution)/shard_map/psum | solution.py:175
  147.9 3.1 fusion.166
  151.9 1.7 fusion.165
  153.6 1.1 fusion.102
  156.0 5.5 %all-to-all-start = ((bf16[8,2,768]{2,1,0:T(2,128)(2,1)}), bf16[8,2,768]{2,1,0:T(2,128)(2,1)S(1)}, u32[]{:S(2)}, u32[]{:S(2)}) async-start(bf16[8,2,768]{2,1,0:T(2,128)(2,1)} %all_to_all.16), calls=%async_computation | async-start | bytes 49152 | tf_op jit(solution)/shard_map/all_to_all | solution.py:195
  161.6 6.6 %all-to-all-done = bf16[8,2,768]{2,1,0:T(2,128)(2,1)S(1)} async-done(((bf16[8,2,768]{2,1,0:T(2,128)(2,1)}), bf16[8,2,768]{2,1,0:T(2,128)(2,1)S(1)}, u32[]{:S(2)}, u32[]{:S(2)}) %all-to-all-start) | async-done | bytes 24608 | tf_op jit(solution)/shard_map/all_to_all | solution.py:195
  173.8 3.3 all-to-all-start.1
  177.4 6.3 %all-to-all-done.1 = bf16[8,2,768]{2,1,0:T(2,128)(2,1)S(1)} async-done(((bf16[8,2,768]{2,1,0:T(2,128)(2,1)}), bf16[8,2,768]{2,1,0:T(2,128)(2,1)S(1)}, u32[]{:S(2)}, u32[]{:S(2)}) %all-to-all-start.1) | async-done | bytes 24608 | tf_op jit(solution)/shard_map/all_to_all | solution.py:210
  184.3 1.5 fusion.110
  186.2 3.2 multiply_reduce_fusion.1
  189.5 1.5 subtract_multiply_fusion.1
  191.7 2.1 copy-done.47
  193.8 2.9 fusion.170
  196.7 1.1 copy-done.49
  197.8 2.6 convolution_convert_fusion
  200.5 5.2 %convolution_convert_fusion.4 = bf16[768,768]{1,0:T(8,128)(2,1)} fusion(bf16[1024,768]{1,0:T(8,128)(2,1)} %copy-done.48, f32[1024,768]{1,0:T(8,128)} %copy-done.10), kind=kOutput, calls=%fused_computation.125 | convolution fusion | flops 1209335808 | bytes 5898240 | tf_op jit(solution)/shard_map/dot_general | solution.py:25
  205.7 3.0 convolution_convert_fusion.5
  208.8 31.1 %all-reduce.15.cloned.1.call-done = bf16[1024,768]{1,0:T(8,128)(2,1)} async-done(((bf16[1024,768]{1,0:T(8,128)(2,1)}), bf16[1024,768]{1,0:T(8,128)(2,1)}) %all-reduce.15.cloned.1.call-update) | async-done | bytes 1572880 | tf_op jit(solution)/shard_map/psum | solution.py:231
  239.9 5.7 %multiply_reduce_fusion.2 = (bf16[768]{0:T(1024)(128)(2,1)S(1)}, f32[1024]{0:T(1024)S(1)}, f32[1024]{0:T(1024)S(1)}, bf16[768]{0:T(1024)(128)(2,1)S(1)}, bf16[768]{0:T(1024)(128)(2,1)}) fusion(f32[1024,768]{1,0:T(8,128)} %copy-done.10, bf16[1024,768]{1,0:T(8,128)(2,1)} %all-reduce.15.cloned.1.call-done, f32[1024]{0:T(1024)S(1)} %add_rsqrt_fusion.1, ...), kind=kLoop, calls=%fused_computation.87 | loop fusion | flops 12578560 | bytes 7891456 | tf_op jit(solution)/shard_map/reduce_sum | solution.py:234
  245.7 2.3 fusion.164
  247.9 1.7 copy-done.5
  254.7 43.6 %while.27 = (s32[]{:T(128)}, bf16[2,512,3,64]{1,3,2,0:T(8,128)(2,1)}, bf16[2,512,3,64]{1,3,2,0:T(8,128)(2,1)}, bf16[2,512,3,64]{1,3,2,0:T(8,128)(2,1)}, bf16[2,5...) while((s32[]{:T(128)}, ...), condition=%wide.region_30.31_spmd, body=%wide.region_28.30_spmd.sunk | while | flops 514625536 | bytes 38954128 | solution.py:243
  254.7 3.6 subtract_exponential_fusion.4
  258.3 2.3 fusion.236
  260.6 6.3 %fusion.238 = bf16[2,512,3,64]{1,3,2,0:T(8,128)(2,1)} fusion(bf16[2,512,3,64]{1,3,2,0:T(8,128)(2,1)} %get-tuple-element.385, s32[]{:T(128)} %get-tuple-element.383, f32[3,512,512]{1,2,0:T(8,128)} %subtract_exponential_fusion.4, f32[3,512,512]{1,2,0:T(8,128)} %fusion.236, bf16[2,512,3,64]{1,3,2,0:T(8,128)(2,1)S(1)} %get-tuple-element.400), kind=kOutput, calls=%fused_computation.43.clone.1 | convolution fusion | flops 104695808 | bytes 12977152 | tf_op jit(solution)/shard_map/while/body/eval_jaxpr/hqk,qhd->khd/dot_general | solution.py:104
  266.9 6.4 %fusion.237 = bf16[2,512,3,64]{1,3,2,0:T(8,128)(2,1)} fusion(bf16[2,512,3,64]{1,3,2,0:T(8,128)(2,1)} %get-tuple-element.384, s32[]{:T(128)} %get-tuple-element.383, f32[3,512,512]{1,2,0:T(8,128)} %subtract_exponential_fusion.4, f32[3,512,512]{1,2,0:T(8,128)} %fusion.236, bf16[2,512,3,64]{1,3,2,0:T(8,128)(2,1)} %get-tuple-element.398), kind=kOutput, calls=%fused_computation.45.clone.1 | convolution fusion | flops 104695808 | bytes 12977152 | tf_op jit(solution)/shard_map/while/body/eval_jaxpr/hqk,khd->qhd/dot_general | solution.py:101
  273.3 3.2 fusion.239
  276.5 3.6 subtract_exponential_fusion.4
  280.1 2.3 fusion.236
  282.4 6.3 %fusion.238 = bf16[2,512,3,64]{1,3,2,0:T(8,128)(2,1)} fusion(bf16[2,512,3,64]{1,3,2,0:T(8,128)(2,1)} %get-tuple-element.385, s32[]{:T(128)} %get-tuple-element.383, f32[3,512,512]{1,2,0:T(8,128)} %subtract_exponential_fusion.4, f32[3,512,512]{1,2,0:T(8,128)} %fusion.236, bf16[2,512,3,64]{1,3,2,0:T(8,128)(2,1)S(1)} %get-tuple-element.400), kind=kOutput, calls=%fused_computation.43.clone.1 | convolution fusion | flops 104695808 | bytes 12977152 | tf_op jit(solution)/shard_map/while/body/eval_jaxpr/hqk,qhd->khd/dot_general | solution.py:104
  288.7 6.4 %fusion.237 = bf16[2,512,3,64]{1,3,2,0:T(8,128)(2,1)} fusion(bf16[2,512,3,64]{1,3,2,0:T(8,128)(2,1)} %get-tuple-element.384, s32[]{:T(128)} %get-tuple-element.383, f32[3,512,512]{1,2,0:T(8,128)} %subtract_exponential_fusion.4, f32[3,512,512]{1,2,0:T(8,128)} %fusion.236, bf16[2,512,3,64]{1,3,2,0:T(8,128)(2,1)} %get-tuple-element.398), kind=kOutput, calls=%fused_computation.45.clone.1 | convolution fusion | flops 104695808 | bytes 12977152 | tf_op jit(solution)/shard_map/while/body/eval_jaxpr/hqk,khd->qhd/dot_general | solution.py:101
  295.1 3.2 fusion.239
  298.3 1.4 copy.69
  299.8 1.2 fusion.100
  303.2 1.8 add_convert_fusion
  305.1 1.2 fusion.101
  306.3 1.2 fusion.99
  307.5 1.2 convolution_convert_fusion.8
  309.2 37.1 %all-reduce.3 = (bf16[192]{0:T(256)(128)(2,1)S(1)}, bf16[192]{0:T(256)(128)(2,1)S(1)}, bf16[768]{0:T(1024)(128)(2,1)S(1)}, bf16[768]{0:T(1024)(128)(2,1)S(1)}, b...) all-reduce(bf16[192]{0:T(256)(128)(2,1)S(1)} %reduce_sum.285, ...), channel_id=1, replica_groups=mesh['dp'=8,'mp'=4] {'dp'}, use_global_device_ids=true, to_apply=%region_34.35 | all-reduce | flops 5760 | bytes 23040 | tf_op jit(solution)/shard_map/psum | solution.py:277
  351.6 4.3 convert_add_fusion
  356.0 139.0 %all-reduce.19.cloned.1.call-done = (bf16[768,192]{0,1:T(8,128)(2,1)}, bf16[768,192]{0,1:T(8,128)(2,1)}, bf16[768,192]{0,1:T(8,128)(2,1)}, bf16[192,768]{1,0:T(8...) async-done(((bf16[768,192]{0,1:T(8,128)(2,1)}, bf16[768,192]{0,1:T(8,128)(2,1)}, bf16[768,192]{0,1:T(8,128)(2,1)}, bf16[192,768]{1,0:T(8,128)(2,1)}, ...) | async-done | bytes 3538960 | tf_op jit(solution)/shard_map/psum | solution.py:276
  495.0 3.0 convert_element_type.276
  498.0 1.6 convert_element_type.279
  (214 shorter events, 32.0 us)
Async XLA Ops:
  7.2 84.0 %copy-start = (bf16[768,768]{1,0:T(8,128)(2,1)S(1)}, bf16[768,768]{1,0:T(8,128)(2,1)}, u32[]{:S(2)}) copy-start(bf16[768,768]{1,0:T(8,128)(2,1)} %param.37) | copy-start | bytes 3538948
  7.2 8.3 %copy-start.2 = (bf16[1024,768]{1,0:T(8,128)(2,1)S(1)}, bf16[1024,768]{1,0:T(8,128)(2,1)}, u32[]{:S(2)}) copy-start(bf16[1024,768]{1,0:T(8,128)(2,1)} %param.24) | copy-start | bytes 4718596
  7.2 8.3 %copy-start.43 = (f32[192]{0:T(256)S(1)}, f32[192]{0:T(256)}, u32[]{:S(2)}) copy-start(f32[192]{0:T(256)} %param.29) | copy-start | bytes 2308
  7.2 80.9 %all-reduce.11.cloned.1.call-start = ((), (), s32[]{:S(2)}) async-start(), calls=%async_computation.2 | async-start | bytes 3145728 | tf_op jit(solution)/shard_map/psum | solution.py:166
  28.7 2.6 copy-start.15
  33.1 2.6 copy-start.15
  37.4 50.7 %copy-start.30 = (f32[768]{0:T(1024)S(1)}, f32[768]{0:T(1024)}, u32[]{:S(2)}) copy-start(f32[768]{0:T(1024)} %param.34) | copy-start | bytes 9220
  38.9 0.8 copy-start.19
  42.4 48.7 %copy-start.32 = (f32[768]{0:T(1024)S(1)}, f32[768]{0:T(1024)}, u32[]{:S(2)}) copy-start(f32[768]{0:T(1024)} %param.35) | copy-start | bytes 9220
  42.4 48.7 %copy-start.38 = (f32[768]{0:T(1024)S(1)}, f32[768]{0:T(1024)}, u32[]{:S(2)}) copy-start(f32[768]{0:T(1024)} %param.36) | copy-start | bytes 9220
  42.5 48.7 %copy-start.42 = (f32[768]{0:T(1024)S(1)}, f32[768]{0:T(1024)}, u32[]{:S(2)}) copy-start(f32[768]{0:T(1024)} %param.38) | copy-start | bytes 9220
  42.5 105.4 %all-reduce.13.cloned.1.call-start = ((), (), s32[]{:S(2)}) async-start(), calls=%async_computation.3 | async-start | bytes 3145728 | tf_op jit(solution)/shard_map/psum | solution.py:175
  88.1 2.1 copy-start.7
  91.2 11.1 %copy-start.40 = (bf16[768,768]{1,0:T(8,128)(2,1)S(1)}, bf16[768,768]{1,0:T(8,128)(2,1)}, u32[]{:S(2)}) copy-start(bf16[768,768]{1,0:T(8,128)(2,1)} %param.39) | copy-start | bytes 3538948
  101.0 1.2 copy-start.48
  102.3 2.6 copy-start.33
  102.3 2.6 copy-start.44
  102.3 2.7 copy-start.45
  102.3 45.6 %copy-start.36 = (f32[768]{0:T(1024)S(1)}, f32[768]{0:T(1024)}, u32[]{:S(2)}) copy-start(f32[768]{0:T(1024)} %param.40) | copy-start | bytes 9220
  151.1 2.5 copy-start.3
  151.1 0.7 copy-start.31
  151.1 0.8 copy-start.37
  156.0 12.1 %all-to-all-start = ((bf16[8,2,768]{2,1,0:T(2,128)(2,1)}), bf16[8,2,768]{2,1,0:T(2,128)(2,1)S(1)}, u32[]{:S(2)}, u32[]{:S(2)}) async-start(bf16[8,2,768]{2,1,0:T(2,128)(2,1)} %all_to_all.16), calls=%async_computation | async-start | bytes 49152 | tf_op jit(solution)/shard_map/all_to_all | solution.py:195
  173.8 9.9 %all-to-all-start.1 = ((bf16[8,2,768]{2,1,0:T(2,128)(2,1)}), bf16[8,2,768]{2,1,0:T(2,128)(2,1)S(1)}, u32[]{:S(2)}, u32[]{:S(2)}) async-start(bf16[8,2,768]{2,1,0:T(2,128)(2,1)} %all_to_all.19), calls=%async_computation.1 | async-start | bytes 49152 | tf_op jit(solution)/shard_map/all_to_all | solution.py:210
  177.2 62.7 %all-reduce.15.cloned.1.call-start = ((), (), s32[]{:S(2)}) async-start(), calls=%async_computation.4 | async-start | bytes 3145728 | tf_op jit(solution)/shard_map/psum | solution.py:231
  184.3 1.9 copy-start.4
  186.2 3.2 copy-start.12
  189.4 1.5 copy-start.41
  189.4 2.2 copy-start.46
  189.4 4.3 copy-start.47
  190.9 5.8 %copy-start.10 = (f32[1024,768]{1,0:T(8,128)}, f32[1024,768]{1,0:T(8,128)S(1)}, u32[]{:S(2)}) copy-start(f32[1024,768]{1,0:T(8,128)S(1)} %subtract_multiply_fusion.1) | copy-start | bytes 9437188
  196.7 1.1 copy-start.49
  200.4 151.2 %all-reduce.17.cloned.1.call-start = ((), (), s32[]{:S(2)}) async-start(), calls=%async_computation.5 | async-start | bytes 3145728 | tf_op jit(solution)/shard_map/psum | solution.py:256
  200.5 5.3 %copy-start.8 = (bf16[1024,768]{1,0:T(8,128)(2,1)S(1)}, bf16[1024,768]{1,0:T(8,128)(2,1)}, u32[]{:S(2)}) copy-start(bf16[1024,768]{1,0:T(8,128)(2,1)} %all-reduce.11.cloned.1.call-done) | copy-start | bytes 4718596
  200.5 5.2 %copy-start.50 = (bf16[1024,768]{1,0:T(8,128)(2,1)S(1)}, bf16[1024,768]{1,0:T(8,128)(2,1)}, u32[]{:S(2)}) copy-start(bf16[1024,768]{1,0:T(8,128)(2,1)} %copy-done.49) | copy-start | bytes 4718596
  239.9 5.7 %copy-start.9 = (bf16[1024,768]{1,0:T(8,128)(2,1)S(1)}, bf16[1024,768]{1,0:T(8,128)(2,1)}, u32[]{:S(2)}) copy-start(bf16[1024,768]{1,0:T(8,128)(2,1)} %all-reduce.11.cloned.1.call-done) | copy-start | bytes 4718596
  239.9 5.7 %copy-start.11 = (f32[1024,768]{1,0:T(8,128)S(1)}, f32[1024,768]{1,0:T(8,128)}, u32[]{:S(2)}) copy-start(f32[1024,768]{1,0:T(8,128)} %copy-done.10) | copy-start | bytes 9437188
  239.9 5.7 %copy-start.13 = (bf16[1024,768]{1,0:T(8,128)(2,1)S(1)}, bf16[1024,768]{1,0:T(8,128)(2,1)}, u32[]{:S(2)}) copy-start(bf16[1024,768]{1,0:T(8,128)(2,1)} %all-reduce.15.cloned.1.call-done) | copy-start | bytes 4718596
  245.6 4.0 copy-start.22
  247.9 1.7 copy-start.5
  249.6 5.1 copy-start.14
  254.7 3.6 copy-start.16
  276.5 3.6 copy-start.16
  298.3 2.7 copy-start.28
  299.8 1.8 copy-start.18
  301.0 1.1 copy-start.17
  301.0 1.6 copy-start.29
  302.1 1.2 copy-start.23
  305.0 2.5 copy-start.20
  305.1 189.9 %all-reduce.19.cloned.1.call-start = ((), (), s32[]{:S(2)}) async-start(), calls=%async_computation.6 | async-start | bytes 7077888 | tf_op jit(solution)/shard_map/psum | solution.py:276
  305.1 2.4 copy-start.6
  307.5 1.7 copy-start.34
  307.5 1.7 copy-start.35
  307.5 1.7 copy-start.39
  495.0 3.0 copy-start.21
  495.0 4.6 copy-start.27
  495.0 5.4 %copy-start.26 = (bf16[768,192]{0,1:T(8,128)(2,1)S(1)}, bf16[768,192]{0,1:T(8,128)(2,1)}, u32[]{:S(2)}) copy-start(bf16[768,192]{0,1:T(8,128)(2,1)} %get-tuple-element.210) | copy-start | bytes 884740
  498.0 3.3 copy-start.25
  498.0 4.2 copy-start.24
  498.0 5.0 copy-start.1
Sparse Core Ops, SparseCore 0:
  42.5 45.5 all-reduce.10
  105.0 42.8 all-reduce.12
  200.6 39.2 all-reduce.14
  305.2 42.8 all-reduce.16
  353.4 141.5 all-reduce.18
where the time goes:
time: 516 us; the launch traced here: 510 us
  waiting for transfers between devices  272 us (53%)
  matrix products  99.3 us (19%)
  other arithmetic  43.5 us (8%)
  blocking collectives  37.1 us (7%)
  local copies, waits for them, and re-layouts  33.9 us (7%)
  between operations  15 us (3%)
  starting transfers between devices  9.44 us (2%)
    psum x1, waiting for transfers between devices, on_device(): lax.psum(g_w_query.astype(jnp.bfloat16), 'dp').astype(jnp.float32)  139 us
    psum x1, waiting for transfers between devices, on_device(): lax.psum(attn_part.astype(jnp.bfloat16), 'mp').astype(jnp.float32)  45.4 us
    psum x1, waiting for transfers between devices, on_device(): lax.psum(ffn_part.astype(jnp.bfloat16), 'mp').astype(jnp.float32)  43 us
    psum x1, blocking collectives, on_device(): lax.psum(g_b_query.astype(jnp.bfloat16), 'dp').astype(jnp.float32)  37.1 us
    psum x1, waiting for transfers between devices, on_device(): lax.psum(times_t(d_up, w_up).astype(jnp.bfloat16), 'mp').astype(jnp.float32)  31.1 us
    dot_general x6, matrix products, t_times(): lax.dot_general(left, right, (((0,), (0,)), ((), ())), preferred_element_...  13 us
    dot_general x2, matrix products, row_grad(): jnp.einsum('hqk,khd->qhd', d_scores, key_row, preferred_element_type=jnp....  12.8 us
    dot_general x2, matrix products, row_grad(): jnp.einsum('hqk,qhd->khd', d_scores, query_row, preferred_element_type=jn...  12.6 us
  transfers between devices with their start and end apart: 7, of which 6 were waited for; matrix products, arithmetic and copies ran while one was open for 4% of the time, Pallas kernels for 0%

commit v1 on v0

v1 whole, which is shorter than its diff:
```python
import functools

import jax
import jax.numpy as jnp
from jax import lax
from jax.experimental import pallas as pl
from jax.experimental.pallas import tpu as pltpu
from jax.sharding import PartitionSpec as P

HEAD_DIM = 64
MAX_PIECE = 128
NEG_FILL = -1e30
NORM_EPS = 1e-12
UNIT_EPS = 1e-06
SIM_SCALE = 50.0
MESH = pl.DeviceIdType.MESH
F32, BF16, I32 = jnp.float32, jnp.bfloat16, jnp.int32
HIGHEST = lax.Precision.HIGHEST


def nn(a, b):
    return lax.dot_general(a, b, (((1,), (0,)), ((), ())), preferred_element_type=F32)


def nt(a, b):
    return lax.dot_general(a, b, (((1,), (1,)), ((), ())), preferred_element_type=F32)


def tn(a, b):
    return lax.dot_general(a, b, (((0,), (0,)), ((), ())), preferred_element_type=F32)


def iota(shape, axis):
    return lax.broadcasted_iota(I32, shape, axis)


def hi_lo(x):
    hi = x.astype(BF16).astype(F32)
    return hi, x - hi


def sizes(n_dp, rows, tokens, width, local, hidden):
    return dict(
        n_dp=n_dp, R=rows, T=tokens, S=tokens // rows, D=width, L=local, F=hidden,
        half=tokens // rows // 2, heads=local // HEAD_DIM,
    )


def layer_kernel(z, names, *refs):
    ref = dict(zip(names, refs))
    g = lambda k: ref[k]
    n_dp, R, S, D, L, F, half, heads = (
        z[k] for k in ("n_dp", "R", "S", "D", "L", "F", "half", "heads")
    )
    T = R * S
    QB = 256 if S % 256 == 0 else S
    n_qb = S // QB
    KB = QB + MAX_PIECE
    CH = D // 128
    dp, mp = lax.axis_index("dp"), lax.axis_index("mp")
    core = mp % 2
    other = 1 - core
    sib = (dp, mp + 1 - 2 * core)
    across = (dp, (mp + 2) % 4)

    bar = pltpu.get_barrier_semaphore()
    for t in (sib, across):
        pl.semaphore_signal(bar, inc=1, device_id=t, device_id_type=MESH)
    for d in range(1, n_dp):
        pl.semaphore_signal(bar, inc=1, device_id=((dp + d) % n_dp, mp), device_id_type=MESH)

    loads = {}
    for i, k in enumerate(("tokens", "wq", "wk", "wv", "wo", "wu", "wd", "og")):
        c = pltpu.make_async_copy(g(k), g(k + "_v"), g("in_sem").at[i])
        c.start()
        loads[k] = c
    pl.semaphore_wait(bar, 1 + n_dp)

    sends = []

    def remote(src, dst, ss, rs, to):
        return pltpu.make_async_remote_copy(
            src_ref=src, dst_ref=dst, send_sem=ss, recv_sem=rs, device_id=to, device_id_type=MESH
        )

    vecs = g("vecs")

    def vec(i, n=None):
        return vecs[i : i + 1, : (n or D)]

    ends = []
    for r in range(R):
        total, row = 0, []
        for p in range(7):
            total = total + g("lengths")[r, p]
            row.append(total)
        ends.append(row)

    def seg_of(position, r):
        seg = jnp.zeros(position.shape, I32)
        for p in range(6):
            seg = seg + jnp.where(position >= ends[r][p], 1, 0)
        return seg

    lane_head = iota((1, L), 1) // HEAD_DIM

    def only_head(x, h):
        return jnp.where(lane_head == h, x, jnp.zeros_like(x))

    def send_half(which, r, compute):
        par = which % 2
        if which >= 2:
            remote(g("asend").at[par, r], g("arecv").at[par, r], g("a_s").at[which - 2, r],
                   g("a_r").at[which - 2, r], sib).wait_send()
        compute(other * half, lambda cols, val: g("asend").__setitem__((par, r, slice(None), cols), val.astype(BF16)))
        c = remote(g("asend").at[par, r], g("arecv").at[par, r], g("a_s").at[which, r], g("a_r").at[which, r], sib)
        c.start()
        compute(core * half, lambda cols, val: g("own").__setitem__((r, slice(None), cols), val))
        if which >= 2:
            sends.append(c)
        return c

    def send_across(which, r, c):
        par = which % 2
        c.wait_recv()
        if which >= 2:
            remote(g("ysend").at[par, r], g("yrecv").at[par, r], g("y_s").at[which - 2, r],
                   g("y_r").at[which - 2, r], across).wait_send()

        def add(i, _):
            rows = pl.ds(pl.multiple_of(i * 64, 64), 64)
            g("ysend")[par, r, rows] = (
                g("own")[r, rows].astype(F32) + g("arecv")[par, r, rows].astype(F32)
            ).astype(BF16)
            return 0

        lax.fori_loop(0, half // 64, add, 0)
        y = remote(g("ysend").at[par, r], g("yrecv").at[par, r], g("y_s").at[which, r], g("y_r").at[which, r], across)
        y.start()
        if which >= 2:
            sends.append(y)
        return y

    def y_total(which, r, rows):
        par = which % 2
        return g("ysend")[par, r, rows].astype(F32) + g("yrecv")[par, r, rows].astype(F32)

    def to_sibling(key, r, i):
        rows = pl.ds(pl.multiple_of(r * S + core * half, half), half)
        c = remote(g(key).at[rows], g(key).at[rows], g("g_s").at[i, r], g("g_r").at[i, r], sib)
        c.start()
        sends.append(c)
        return c

    TR = 32

    def by_rows(fn):
        def body(i, _):
            fn(pl.ds(pl.multiple_of(i * TR, TR), TR), i * TR)
            return 0

        lax.fori_loop(0, half // TR, body, 0)

    def fold(x):
        return jnp.sum(x.reshape(x.shape[0] // 8, 8, x.shape[1]), axis=0)

    def row_ds(r, start, n):
        return pl.ds(pl.multiple_of(r * S + core * half + start, TR), n)

    def project(r):
        rows = pl.ds(r * S, S)
        x = g("tokens_v")[rows, :]
        g("q")[rows, :] = ((nn(x, g("wq_v")[...]) + vec(0, L)).astype(BF16) * (HEAD_DIM**-0.5)).astype(BF16)
        g("k")[rows, :] = nn(x, g("wk_v")[...]).astype(BF16)
        g("v")[rows, :] = (nn(x, g("wv_v")[...]) + vec(1, L)).astype(BF16)

    def window(b):
        return min(max(b * QB - MAX_PIECE, 0), S - KB) if KB < S else 0

    KW = min(KB, S)
    if n_qb > 2:
        KW = min(QB + 2 * MAX_PIECE, S)

    def win(b):
        return min(max(b * QB - MAX_PIECE, 0), S - KW)

    def attend(r):
        for b in range(n_qb):
            q0, k0 = r * S + b * QB, r * S + win(b)
            same = seg_of(iota((QB, 1), 0) + b * QB, r) == seg_of(iota((1, KW), 1) + win(b), r)
            qb = g("q")[q0 : q0 + QB, :]
            kb = g("k")[k0 : k0 + KW, :]
            vb = g("v")[k0 : k0 + KW, :]
            ctx = None
            for h in range(heads):
                s = jnp.where(same, nt(only_head(qb, h), kb), NEG_FILL)
                e = jnp.exp(s - jnp.max(s, axis=-1, keepdims=True))
                p = (e * (1.0 / jnp.sum(e, axis=-1, keepdims=True))).astype(BF16)
                g("probs")[(r * n_qb + b) * heads + h] = p
                c = nn(p, only_head(vb, h))
                ctx = c if ctx is None else ctx + c
            g("ctx")[q0 : q0 + QB, :] = ctx.astype(BF16)

    def attn_out(r):
        def compute(start, put):
            x = g("ctx")[pl.ds(pl.multiple_of(r * S + start, half), half), :]
            for n in range(D // 256):
                put(slice(n * 256, n * 256 + 256), nn(x, g("wo_v")[:, n * 256 : n * 256 + 256]))

        return compute

    def norm(v):
        mean = jnp.mean(v, axis=-1, keepdims=True)
        c = v - mean
        rstd = lax.rsqrt(jnp.mean(c * c, axis=-1, keepdims=True) + NORM_EPS)
        return c * rstd, rstd

    def first_norm(r):
        def body(rows, start):
            mine = row_ds(r, start, TR)
            xh, rstd = norm(g("tokens_v")[mine].astype(F32) + y_total(0, r, rows) + vec(2))
            g("xhat1")[r, rows] = xh
            g("rstd1")[r, rows] = rstd
            h = xh * vec(3) + vec(4)
            g("hid")[r, rows] = h
            g("hl")[mine] = h.astype(BF16)

        by_rows(body)

    FM = 256
    FT = 256

    def ffn_up(r):
        def body(i, _):
            rows = pl.ds(pl.multiple_of(r * S + i * FM, FM), FM)
            x = g("hl")[rows, :]
            for n in range(F // FT):
                cols = slice(n * FT, n * FT + FT)
                u = nn(x, g("wu_v")[:, cols]) + vecs[5:6, cols]
                phi = 0.5 + 0.5 * lax.erf(u * 0.7071067811865476)
                g("act")[rows, cols] = (u * phi).astype(BF16)
                g("gp")[rows, cols] = (phi + u * (jnp.exp(-0.5 * (u * u)) * 0.3989422804014327)).astype(BF16)
            return 0

        lax.fori_loop(0, S // FM, body, 0)

    def ffn_down(r):
        def compute(start, put):
            x = g("act")[pl.ds(pl.multiple_of(r * S + start, half), half), :]
            for n in range(D // 256):
                put(slice(n * 256, n * 256 + 256), nn(x, g("wd_v")[:, n * 256 : n * 256 + 256]))

        return compute

    def second_norm(r):
        lane = iota((8, TR), 1)
        piece = iota((8, TR), 0)

        def body(rows, start):
            xh, rstd = norm(g("hid")[r, rows] + y_total(1, r, rows) + vec(6))
            g("xhat2")[r, rows] = xh
            g("rstd2")[r, rows] = rstd
            res = xh * vec(7) + vec(8)
            low = res.astype(BF16)
            g("res")[row_ds(r, start, TR)] = low
            seg = seg_of(lane + (core * half + start), r)
            member = jnp.where((seg == piece) & (piece < 6), 1.0, 0.0).astype(BF16)
            rest = (res - low.astype(F32)).astype(BF16)
            at = slice(r * 8, r * 8 + 8)
            g("pool")[at, :] = g("pool")[at, :] + nn(member, low) + nn(member, rest)

        by_rows(body)

    PR = 16
    n_sent = R * 6

    def per_row(values, axis, shape, fill):
        pos = iota(shape, axis) % PR
        out = jnp.full(shape, fill, I32)
        for s in range(n_sent):
            out = jnp.where(pos == (s // 6) * 8 + s % 6, values[s], out)
        return out

    def slot_onehot(axis):
        shape = (n_dp * 16, CH * PR) if axis == 1 else (CH * PR, n_dp * 16)
        line = (1, CH * PR) if axis == 1 else (CH * PR, 1)
        vals = [g("send_slot")[s] // 2 * 16 + g("send_slot")[s] % 2 for s in range(n_sent)]
        target = per_row(vals, axis if axis == 1 else 0, line, -65536) + iota(line, 1 if axis == 1 else 0) // PR * 2
        return jnp.where(iota(shape, 0 if axis == 1 else 1) == target, 1.0, 0.0).astype(BF16)

    def place_onehot(axis):
        line = (1, n_dp * 16) if axis == 1 else (n_dp * 16, 1)
        shape = (CH * PR, n_dp * 16) if axis == 1 else (n_dp * 16, CH * PR)
        pos = iota(line, axis)
        slot = pos // 16 * 2 + pos % 2
        target = jnp.zeros(line, I32)
        for s in range(2 * n_dp):
            target = jnp.where(slot == s, g("recv_place")[s], target)
        target = target + pos % 16 // 2 * PR
        return jnp.where(iota(shape, 0 if axis == 1 else 1) == target, 1.0, 0.0).astype(BF16)

    def stack(x):
        return jnp.concatenate([x[:, c * 128 : c * 128 + 128] for c in range(CH)], axis=0)

    def unstack(x):
        return jnp.concatenate([x[c * PR : c * PR + PR] for c in range(CH)], axis=1)

    def peers(src, dst, ssem, rsem):
        cs = []
        mine = pl.ds(pl.multiple_of(dp * 16, 16), 16)
        for d in range(1, n_dp):
            t = (dp + d) % n_dp
            c = remote(src.at[pl.ds(pl.multiple_of(t * 16, 16), 16)], dst.at[mine], ssem.at[d], rsem.at[d], (t, mp))
            c.start()
            cs.append(c)
            sends.append(c)
        dst[mine] = src[mine]
        for c in cs:
            c.wait_recv()

    def pairs():
        c = remote(g("pool"), g("pool_r"), g("pool_sem").at[0], g("pool_sem").at[1], sib)
        c.start()
        lens = [g("lengths")[s // 6, s % 6] for s in range(n_sent)]
        size = per_row(lens, 0, (PR, 1), 1).astype(F32)
        inv = 1.0 / size
        hot = slot_onehot(1)
        c.wait()
        pooled = (g("pool")[...] + g("pool_r")[...]) * inv
        g("outg")[...] = nn(hot, stack(pooled).astype(BF16)).astype(BF16)
        peers(g("outg"), g("inc"), g("p_s").at[0], g("p_r").at[0])
        o = unstack(nn(place_onehot(1), g("inc")[...]))
        s = lax.rsqrt(jnp.sum(o * o, axis=-1, keepdims=True) + UNIT_EPS)
        u = o * s
        logits = SIM_SCALE * lax.dot_general(
            u, u, (((1,), (1,)), ((), ())), precision=HIGHEST, preferred_element_type=F32
        )
        i, j = iota((PR, PR), 0), iota((PR, PR), 1)
        live = (i % 2 == 0) & (i < n_sent) & (j % 2 == 1) & (j < n_sent)
        lm = jnp.where(live, logits, NEG_FILL)
        peak = jnp.max(lm, axis=-1, keepdims=True)
        e = jnp.where(live, jnp.exp(lm - peak), 0.0)
        tot = jnp.maximum(jnp.sum(e, axis=-1, keepdims=True), 1e-30)
        partner = live & (j == i + 1)
        loss = peak + jnp.log(tot) - jnp.sum(jnp.where(partner, logits, 0.0), axis=-1, keepdims=True)
        i2, j2 = iota((PR, 128), 0), iota((PR, 128), 1)
        g("loss_v")[...] = jnp.broadcast_to(
            jnp.sum(jnp.where((i2 == 2 * j2) & (i2 < n_sent), loss, 0.0), axis=0, keepdims=True), (8, 128)
        )
        dl = e / tot - jnp.where(partner, 1.0, 0.0)
        du = SIM_SCALE * (
            lax.dot_general(dl, u, (((1,), (0,)), ((), ())), precision=HIGHEST, preferred_element_type=F32)
            + lax.dot_general(dl, u, (((0,), (0,)), ((), ())), precision=HIGHEST, preferred_element_type=F32)
        )
        do = s * (du - u * jnp.sum(u * du, axis=-1, keepdims=True))
        g("outg2")[...] = nn(place_onehot(0), stack(do).astype(BF16)).astype(BF16)
        peers(g("outg2"), g("inc2"), g("p_s").at[1], g("p_r").at[1])
        g("dpool")[...] = unstack(nn(slot_onehot(0), g("inc2")[...])) * inv

    def norm_back(dx, xh, rstd):
        return rstd * (
            dx - jnp.mean(dx, axis=-1, keepdims=True) - xh * jnp.mean(dx * xh, axis=-1, keepdims=True)
        )

    def second_norm_back(r):
        hi, lo = hi_lo(g("dpool")[r * 8 : r * 8 + 8, :])
        rhs = jnp.concatenate([hi, lo], axis=0).astype(BF16)
        lane = iota((TR, 16), 1) % 8

        def body(rows, start):
            mine = row_ds(r, start, TR)
            seg = seg_of(iota((TR, 1), 0) + (core * half + start), r)
            member = jnp.where((seg == lane) & (lane < 6), 1.0, 0.0).astype(BF16)
            d = g("og_v")[mine].astype(F32) + nn(member, rhs)
            xh = g("xhat2")[r, rows]
            g("acc")[4] += fold(d * xh)
            g("acc")[5] += fold(d)
            d2 = norm_back(d * vec(7), xh, g("rstd2")[r, rows])
            g("acc")[3] += fold(d2)
            g("d2")[r, rows] = d2
            g("d2l")[mine] = d2.astype(BF16)

        by_rows(body)

    def ffn_back(r):
        def body(i, _):
            rows = pl.ds(pl.multiple_of(r * S + i * FM, FM), FM)
            x = g("d2l")[rows, :]
            for n in range(F // FT):
                cols = slice(n * FT, n * FT + FT)
                da = nt(x, g("wd_v")[cols, :]).astype(BF16)
                du = (da.astype(F32) * g("gp")[rows, cols].astype(F32)).astype(BF16)
                g("dup")[rows, cols] = du
                g("acc")[6, :, cols] += fold(du.astype(F32))
            return 0

        lax.fori_loop(0, S // FM, body, 0)

    def ffn_back_out(r):
        def compute(start, put):
            x = g("dup")[pl.ds(pl.multiple_of(r * S + start, half), half), :]
            for n in range(D // 256):
                put(slice(n * 256, n * 256 + 256), nt(x, g("wu_v")[n * 256 : n * 256 + 256, :]))

        return compute

    def ffn_weights():
        for n in range(F // 256):
            g("grad")[0, n * 256 : n * 256 + 256, :] = tn(g("act")[:, n * 256 : n * 256 + 256], g("d2l")[...]).astype(BF16)
        for n in range(D // 256):
            g("grad")[1, n * 256 : n * 256 + 256, :] = tn(g("hl")[:, n * 256 : n * 256 + 256], g("dup")[...]).astype(BF16)

    def first_norm_back(r):
        def body(rows, start):
            mine = row_ds(r, start, TR)
            d = g("d2")[r, rows] + y_total(2, r, rows)
            xh = g("xhat1")[r, rows]
            g("acc")[1] += fold(d * xh)
            g("acc")[2] += fold(d)
            d1 = norm_back(d * vec(3), xh, g("rstd1")[r, rows])
            g("acc")[0] += fold(d1)
            g("d1")[r, rows] = d1
            g("d1l")[mine] = d1.astype(BF16)

        by_rows(body)

    def attend_back(r):
        rows = pl.ds(r * S, S)
        g("dctx")[rows, :] = nt(g("d1l")[rows, :], g("wo_v")[...]).astype(BF16)
        g("dk_acc")[...] = jnp.zeros((S, L), F32)
        g("dv_acc")[...] = jnp.zeros((S, L), F32)
        for b in range(n_qb):
            q0, k0 = r * S + b * QB, r * S + win(b)
            qb = g("q")[q0 : q0 + QB, :]
            cb = g("dctx")[q0 : q0 + QB, :]
            kb = g("k")[k0 : k0 + KW, :]
            vb = g("v")[k0 : k0 + KW, :]
            dq = dk = dv = None
            for h in range(heads):
                p = g("probs")[(r * n_qb + b) * heads + h]
                dp_ = nt(cb, only_head(vb, h))
                pf = p.astype(F32)
                delta = jnp.sum(pf * dp_, axis=-1, keepdims=True)
                ds = (pf * (dp_ - delta)).astype(BF16)
                a, c, e = nn(ds, only_head(kb, h)), tn(ds, only_head(qb, h)), tn(p, only_head(cb, h))
                dq, dk, dv = (a, c, e) if dq is None else (dq + a, dk + c, dv + e)
            g("dq")[q0 : q0 + QB, :] = (dq * (HEAD_DIM**-0.5)).astype(BF16)
            g("dk_acc")[win(b) : win(b) + KW, :] += dk
            g("dv_acc")[win(b) : win(b) + KW, :] += dv
        g("dk")[rows, :] = g("dk_acc")[...].astype(BF16)
        g("dv")[rows, :] = g("dv_acc")[...].astype(BF16)
        g("acc")[7, :, :L] += fold(g("dq")[rows, :].astype(F32))
        g("acc")[8, :, :L] += fold(g("dv")[rows, :].astype(F32))

    def attend_back_out(r):
        def compute(start, put):
            at = pl.ds(pl.multiple_of(r * S + start, half), half)
            for n in range(D // 256):
                w = slice(n * 256, n * 256 + 256)
                put(
                    w,
                    nt(g("dq")[at, :], g("wq_v")[w, :])
                    + nt(g("dk")[at, :], g("wk_v")[w, :])
                    + nt(g("dv")[at, :], g("wv_v")[w, :]),
                )

        return compute

    def attend_weights():
        for i, k in enumerate(("dq", "dk", "dv")):
            g("grad")[2, i * L : i * L + L, :] = tn(g(k)[...], g("tokens_v")[...]).astype(BF16)
        g("grad")[2, 3 * L : 4 * L, :] = tn(g("ctx")[...], g("d1l")[...]).astype(BF16)

    def finish(r):
        def body(rows, start):
            g("tg")[row_ds(r, start, TR)] = g("d1")[r, rows] + y_total(3, r, rows)

        by_rows(body)

    xi, zi = dp % 2, dp // 2
    nz = n_dp // 2
    in_kernel = z["in_kernel"]
    outer = (zi == 0) | (zi == nz - 1)
    inner = (zi != 0) & (zi != nz - 1)
    xp = (dp + 1 - 2 * xi, mp)
    zp = (dp + 2 - 4 * (zi % 2), mp)
    zq = ((dp + 2 * (3 - 2 * zi)) % n_dp if in_kernel else dp, mp)
    ii = zi // 2
    grad, gsum = g("grad"), g("gsum")

    def add_into(dst, dst_at, a, a_at, b, b_at, n):
        step = 48 if n % 48 == 0 else 16

        def body(i, _):
            o = i * step
            x = a[a_at[0], pl.ds(pl.multiple_of(a_at[1] + o, 16), step), :].astype(F32)
            y = b[b_at[0], pl.ds(pl.multiple_of(b_at[1] + o, 16), step), :].astype(F32)
            dst[dst_at[0], pl.ds(pl.multiple_of(dst_at[1] + o, 16), step), :] = (x + y).astype(BF16)
            return 0

        lax.fori_loop(0, n // step, body, 0)

    def x_job(slot, j, r0, n):
        h = n // 2
        mine = pl.multiple_of(r0 + xi * h, 16)
        yours = pl.multiple_of(r0 + (1 - xi) * h, 16)
        own, theirs = pl.ds(mine, h), pl.ds(yours, h)
        s = lambda k: g("d_s").at[slot, k]
        q = lambda k: g("d_r").at[slot, k]
        buf = g("rx")
        x1 = remote(grad.at[j, theirs], buf.at[slot * 3], s(0), q(0), xp)
        z1 = remote(grad.at[j, own], buf.at[slot * 3 + 1], s(1), q(1), zp)
        z2 = remote(grad.at[j, own], buf.at[slot * 3 + 2], s(2), q(2), zq)
        z3 = remote(gsum.at[j, own], gsum.at[j, own], s(3), q(3), zp)
        x2 = remote(gsum.at[j, own], gsum.at[j, own], s(4), q(4), xp)

        def st0():
            x1.start()

        def st1():
            x1.wait_recv()
            add_into(grad, (j, mine), grad, (j, mine), buf, (slot * 3, 0), h)
            pl.when(outer)(z1.start)

        def st2():
            @pl.when(inner)
            def _():
                z1.wait_recv()
                add_into(grad, (j, mine), grad, (j, mine), buf, (slot * 3 + 1, 0), h)
                z2.start()

        def st3():
            @pl.when(inner)
            def _():
                z2.wait_recv()
                add_into(gsum, (j, mine), grad, (j, mine), buf, (slot * 3 + 2, 0), h)
                z3.start()
                x2.start()

        def st4():
            @pl.when(outer)
            def _():
                z3.wait_recv()
                x2.start()

        def st5():
            x2.wait_recv()

        def end():
            x1.wait_send()
            x2.wait_send()

            @pl.when(outer)
            def _():
                z1.wait_send()

            @pl.when(inner)
            def _():
                z2.wait_send()
                z3.wait_send()

        return [st0, st1, st2, st3, st4, st5], end

    def z_job(slot, j, r0, n):
        h = n // 2
        mine = pl.multiple_of(r0 + ii * h, 16)
        yours = pl.multiple_of(r0 + (1 - ii) * h, 16)
        own, theirs, whole = pl.ds(mine, h), pl.ds(yours, h), pl.ds(r0, n)
        s = lambda k: g("d_s").at[slot, k]
        q = lambda k: g("d_r").at[slot, k]
        buf, big = g("rx"), g("rz")
        z1 = remote(grad.at[j, whole], big.at[slot], s(0), q(0), zp)
        z2 = remote(grad.at[j, theirs], buf.at[slot * 3], s(1), q(1), zq)
        x = remote(grad.at[j, own], buf.at[slot * 3 + 1], s(2), q(2), xp)
        z2b = remote(gsum.at[j, own], gsum.at[j, own], s(3), q(3), zq)
        z3a = remote(gsum.at[j, own], gsum.at[j, own], s(4), q(4), zp)
        z3b = remote(gsum.at[j, theirs], gsum.at[j, theirs], s(5), q(5), zp)

        def st0():
            pl.when(outer)(z1.start)

        def st1():
            @pl.when(inner)
            def _():
                z1.wait_recv()
                add_into(grad, (j, r0), grad, (j, r0), big, (slot, 0), n)
                z2.start()

        def st2():
            @pl.when(inner)
            def _():
                z2.wait_recv()
                add_into(grad, (j, mine), grad, (j, mine), buf, (slot * 3, 0), h)
                x.start()

        def st3():
            @pl.when(inner)
            def _():
                x.wait_recv()
                add_into(gsum, (j, mine), grad, (j, mine), buf, (slot * 3 + 1, 0), h)
                z2b.start()
                z3a.start()

        def st4():
            @pl.when(inner)
            def _():
                z2b.wait_recv()
                z3b.start()

        def st5():
            @pl.when(outer)
            def _():
                z3a.wait_recv()
                z3b.wait_recv()

        def end():
            @pl.when(outer)
            def _():
                z1.wait_send()

            @pl.when(inner)
            def _():
                for c in (z2, x, z2b, z3a, z3b):
                    c.wait_send()

        return [st0, st1, st2, st3, st4, st5], end

    n_sub = z["n_sub"]
    sub = D // n_sub

    def jobs_of(j):
        made = []
        for i in range(n_sub):
            kind = x_job if i % 2 == 0 else z_job
            made.append(kind(j * n_sub + i, j, i * sub, sub))
        return made

    g("pool")[...] = jnp.zeros((PR, D), F32)
    g("acc")[...] = jnp.zeros(g("acc").shape, F32)
    for k in ("tokens", "wq", "wk", "wv"):
        loads[k].wait()
    a, y = {}, {}
    for r in range(R):
        project(r)
        attend(r)
        if r == 0:
            loads["wo"].wait()
        if r > 0:
            y[0, r - 1] = send_across(0, r - 1, a[0, r - 1])
        a[0, r] = send_half(0, r, attn_out(r))
    y[0, R - 1] = send_across(0, R - 1, a[0, R - 1])
    for k in ("wu", "wd", "og"):
        loads[k].wait()
    for r in range(R):
        y[0, r].wait_recv()
        first_norm(r)
        c = to_sibling("hl", r, 0)
        if r > 0:
            y[1, r - 1] = send_across(1, r - 1, a[1, r - 1])
        c.wait_recv()
        ffn_up(r)
        a[1, r] = send_half(1, r, ffn_down(r))
    y[1, R - 1] = send_across(1, R - 1, a[1, R - 1])
    out_c = []
    for r in range(R):
        y[1, r].wait_recv()
        second_norm(r)
        out_c.append(to_sibling("res", r, 1))
    pairs()
    cs = []
    for r in range(R):
        second_norm_back(r)
        cs.append(to_sibling("d2l", r, 2))
    for c in out_c:
        c.wait_recv()
    outs = [pltpu.make_async_copy(g("res"), g("res_o"), g("out_sem").at[0])]
    outs[-1].start()
    for r in range(R):
        cs[r].wait_recv()
        ffn_back(r)
        if r > 0:
            y[2, r - 1] = send_across(2, r - 1, a[2, r - 1])
        a[2, r] = send_half(2, r, ffn_back_out(r))
    y[2, R - 1] = send_across(2, R - 1, a[2, R - 1])
    ffn_weights()
    for r in range(R):
        y[2, r].wait_recv()
        first_norm_back(r)
        c = to_sibling("d1l", r, 3)
        c.wait_recv()
        attend_back(r)
        a[3, r] = send_half(3, r, attend_back_out(r))
        y[3, r] = send_across(3, r, a[3, r])
    attend_weights()
    fin = []
    for r in range(R):
        y[3, r].wait_recv()
        finish(r)
        fin.append(to_sibling("tg", r, 4))

    for k in range(7):
        g("vmine")[k : k + 1, :] = jnp.sum(g("acc")[k], axis=0, keepdims=True)
    g("vmine")[7:8, :] = jnp.zeros((1, D), F32)
    g("vmine")[7:8, 0:L] = jnp.sum(g("acc")[7], axis=0, keepdims=True)[:, :L]
    g("vmine")[7:8, 256 : 256 + L] = jnp.sum(g("acc")[8], axis=0, keepdims=True)[:, :L]
    c = remote(g("vmine"), g("vsib"), g("pool_sem").at[2], g("pool_sem").at[3], sib)
    c.start()
    c.wait()
    v = g("vmine")[...] + jnp.where(iota((8, D), 0) < 6, g("vsib")[...], 0.0)
    g("vall")[dp] = v
    vs = []
    for d in range(1, n_dp):
        t = (dp + d) % n_dp
        c = remote(g("vall").at[dp], g("vall").at[dp], g("v_s").at[d], g("v_r").at[d], (t, mp))
        c.start()
        vs.append(c)
        sends.append(c)

    if in_kernel:
        jobs = [job for j in range(3) for job in jobs_of(j)]
        depth = 6
        for wave in range(len(jobs) // 2 + depth):
            for i in range(len(jobs)):
                st = wave - i // 2
                if 0 <= st < depth:
                    jobs[i][0][st]()
        for _, end in jobs:
            end()
    else:
        gsum = grad

    for c in fin:
        c.wait_recv()
    for i, (k, o) in enumerate(((g("tg"), "tg_o"), (gsum, "g_o"), (g("loss_v"), "loss_o"))):
        outs.append(pltpu.make_async_copy(k, g(o), g("out_sem").at[1 + i]))
        outs[-1].start()
    for c in vs:
        c.wait_recv()
    v = g("vall")[0]
    for d in range(1, n_dp):
        v = v + g("vall")[d]
    g("vout")[...] = v
    outs.append(pltpu.make_async_copy(g("vout"), g("vec_o"), g("out_sem").at[4]))
    outs[-1].start()
    for c in sends:
        c.wait_send()
    for c in outs:
        c.wait()


def on_device(n_dp, tokens, lengths, send_slot, recv_place, w_query, b_query, w_key, w_value, b_value, w_out,
              output_bias, first_norm_gain, first_norm_bias, w_up, b_up, w_down, down_bias, second_norm_gain,
              second_norm_bias, out_grad):
    T, D = tokens.shape
    R, L, F = lengths.shape[0], w_query.shape[1], w_up.shape[1]
    z = sizes(n_dp, R, T, D, L, F)
    S, half, heads = z["S"], z["half"], z["heads"]
    z["in_kernel"] = n_dp == 8
    z["n_sub"] = 8
    n_jobs = 3 * z["n_sub"]
    sub = D // z["n_sub"]
    widen = lambda v: jnp.pad(v, (0, D - v.shape[0]))
    vecs = jnp.stack([
        widen(b_query), widen(b_value), output_bias, first_norm_gain, first_norm_bias, b_up, down_bias,
        second_norm_gain, second_norm_bias,
    ])
    ins = dict(lengths=lengths, send_slot=send_slot, recv_place=recv_place, vecs=vecs, tokens=tokens, wq=w_query,
               wk=w_key, wv=w_value, wo=w_out, wu=w_up, wd=w_down, og=out_grad)
    any_, vmem, smem = pl.BlockSpec(memory_space=pl.ANY), pl.BlockSpec(memory_space=pltpu.VMEM), pl.BlockSpec(memory_space=pltpu.SMEM)
    in_specs = [smem] * 3 + [vmem] + [any_] * 8
    outs = dict(
        res_o=((T, D), BF16), tg_o=((T, D), F32), g_o=((3, D, D), BF16), vec_o=((8, D), F32), loss_o=((8, 128), F32)
    )
    n_qb = S // 256
    KW = min(256 + (MAX_PIECE if n_qb <= 2 else 2 * MAX_PIECE), S)
    V = pltpu.VMEM
    dma = pltpu.SemaphoreType.DMA
    scratch = dict(
        tokens_v=V((T, D), BF16), og_v=V((T, D), BF16), wq_v=V((D, L), BF16), wk_v=V((D, L), BF16),
        wv_v=V((D, L), BF16), wo_v=V((L, D), BF16), wu_v=V((D, F), BF16), wd_v=V((F, D), BF16),
        q=V((T, L), BF16), k=V((T, L), BF16), v=V((T, L), BF16), ctx=V((T, L), BF16), dctx=V((T, L), BF16),
        dq=V((T, L), BF16), dk=V((T, L), BF16), dv=V((T, L), BF16), dk_acc=V((S, L), F32), dv_acc=V((S, L), F32),
        probs=V((R * n_qb * heads, 256, KW), BF16),
        xhat1=V((R, half, D), F32), xhat2=V((R, half, D), F32), hid=V((R, half, D), F32), d2=V((R, half, D), F32),
        d1=V((R, half, D), F32), rstd1=V((R, half, 1), F32), rstd2=V((R, half, 1), F32),
        hl=V((T, D), BF16), act=V((T, F), BF16), gp=V((T, F), BF16), d2l=V((T, D), BF16), dup=V((T, F), BF16),
        d1l=V((T, D), BF16), res=V((T, D), BF16), tg=V((T, D), F32),
        asend=V((2, R, half, D), BF16), arecv=V((2, R, half, D), BF16), own=V((R, half, D), F32),
        ysend=V((2, R, half, D), BF16), yrecv=V((2, R, half, D), BF16),
        pool=V((16, D), F32), pool_r=V((16, D), F32), dpool=V((16, D), F32), acc=V((9, 8, D), F32),
        outg=V((n_dp * 16, 128), BF16), inc=V((n_dp * 16, 128), BF16), outg2=V((n_dp * 16, 128), BF16),
        inc2=V((n_dp * 16, 128), BF16), loss_v=V((8, 128), F32),
        vmine=V((8, D), F32), vsib=V((8, D), F32), vall=V((n_dp, 8, D), F32), vout=V((8, D), F32),
        grad=V((3, D, D), BF16), gsum=V((3, D, D), BF16), rx=V((n_jobs * 3, sub // 2, D), BF16),
        rz=V((n_jobs, sub, D), BF16),
        in_sem=dma((8,)), out_sem=dma((5,)), a_s=dma((4, R)), a_r=dma((4, R)), y_s=dma((4, R)), y_r=dma((4, R)),
        g_s=dma((5, R)), g_r=dma((5, R)), pool_sem=dma((4,)), p_s=dma((2, n_dp)), p_r=dma((2, n_dp)),
        v_s=dma((n_dp,)), v_r=dma((n_dp,)), d_s=dma((n_jobs, 6)), d_r=dma((n_jobs, 6)),
    )
    names = tuple(ins) + tuple(outs) + tuple(scratch)
    res, tg, grads, vec, loss = pl.pallas_call(
        functools.partial(layer_kernel, z, names),
        out_shape=[jax.ShapeDtypeStruct(*s) for s in outs.values()],
        in_specs=in_specs,
        out_specs=[any_] * 5,
        scratch_shapes=list(scratch.values()),
        compiler_params=pltpu.CompilerParams(
            collective_id=0, has_side_effects=True, vmem_limit_bytes=63 * 2**20
        ),
    )(*ins.values())
    if not z["in_kernel"]:
        grads = lax.psum(grads, "dp")
    gd, gu, ga = grads[0].astype(F32), grads[1].astype(F32), grads[2].astype(F32)
    return (
        res, loss[0, : R * 3], tg, ga[:L].T, vec[7, :L], ga[L : 2 * L].T, ga[2 * L : 3 * L].T, vec[7, 256 : 256 + L],
        ga[3 * L :], vec[0], vec[1], vec[2], gu, vec[6], gd, vec[3], vec[4], vec[5],
    )


def solution(mesh):
    rows, flat, cut = P("dp", None), P("dp"), P("mp")
    across, down = P(None, "mp"), P("mp", None)
    return jax.shard_map(
        functools.partial(on_device, mesh.shape["dp"]),
        mesh=mesh,
        in_specs=(rows, rows, flat, flat, across, cut, across, across, cut, down, P(), P(), P(), across, cut, down,
                  P(), P(), P(), rows),
        out_specs=(rows, flat, rows, across, cut, across, across, cut, down, P(), P(), P(), across, cut, down, P(),
                   P(), P()),
        check_vma=False,
    )
```

time: 516 us -> 226 us (0.44)
  waiting for transfers between devices: 272 us -> 0 us
  Pallas kernels: 0 us -> 200 us
  matrix products: 99.3 us -> 0 us
  other arithmetic: 43.5 us -> 4.62 us
  blocking collectives: 37.1 us -> 0 us
  between operations: 15 us -> 0.68 us
  local copies, waits for them, and re-layouts: 33.9 us -> 19.8 us
  starting transfers between devices: 9.44 us -> 0 us
    psum x5 -> x0, waiting for transfers between devices: 259 us -> none  [the longest x1 139 us: on_device(): lax.psum(g_w_query.astype(jnp.bfloat16), 'dp').astype(jnp.float32)]
    pallas_call x0 -> x1, Pallas kernels: none -> 200 us  [on_device(): pl.pallas_call(functools.partial(layer_kernel, z, names), out_shape=[jax....]
    dot_general x37 -> x0, matrix products: 99.3 us -> none  [the longest x6 13 us: t_times(): lax.dot_general(left, right, (((0,), (0,)), ((), ())), preferred_element_...]
    psum x1 -> x0, blocking collectives: 37.1 us -> none  [on_device(): lax.psum(g_b_query.astype(jnp.bfloat16), 'dp').astype(jnp.float32)]
    reduce_sum x15 -> x0, other arithmetic: 19.7 us -> none  [the longest x1 5.72 us: on_device(): jnp.sum(hidden_gradient * first_normalized_rows, axis=0)]
    all_to_all x2 -> x0, waiting for transfers between devices: 12.9 us -> none  [the longest x1 6.62 us: on_device(): lax.all_to_all(outgoing, 'dp', split_axis=0, concat_axis=0, tiled=True)]
    convert_element_type x18 -> x1, other arithmetic: 15 us -> 4.62 us  [on_device(): grads[0].astype(F32)]
    while x16 -> x0, local copies, waits for them, and re-layouts: 10.1 us -> none  [the longest x4 6.78 us: on_device(): lax.map(row_attend, (query_rows, key_rows, value_rows, same_piece))]
  transfers between devices with their start and end apart: 7 -> 0, of which waited for: 6 -> 0; matrix products, arithmetic and copies ran while one was open for 4% -> 0% of each run, Pallas kernels for 0% -> 0%
where the time goes in v1:
time: 226 us; the launch traced here: 225 us
  Pallas kernels  200 us (88%)
  local copies, waits for them, and re-layouts  19.8 us (9%)
  other arithmetic  4.62 us (2%)
    pallas_call x1, Pallas kernels, on_device(): pl.pallas_call(functools.partial(layer_kernel, z, names), out_shape=[jax....  200 us
    unnamed x11, local copies, waits for them, and re-layouts  8.45 us
    another operation x10, local copies, waits for them, and re-layouts, on_device(): jnp.stack([widen(b_query), widen(b_value), output_bias, first_norm_gain,...  6.1 us
    convert_element_type x1, other arithmetic, on_device(): grads[0].astype(F32)  4.62 us

profile of v1, /device:TPU:0, one launch (start us, length us, event | category | flops | bytes accessed | tf_op | source)
XLA Modules:
  0.0 225.0 jit_solution(3659030068445441177)
XLA Ops:
  0.7 0.7 pad.7
  1.3 0.7 pad.8
  2.0 0.7 stack.32
  2.7 0.7 stack.33
  3.4 0.7 stack.34
  4.1 0.7 stack.35
  4.8 0.7 stack.36
  5.5 0.7 stack.37
  6.2 0.7 stack.38
  6.9 1.3 stack.39.refs_3_
  8.1 1.9 copy.38.refs_5_
  10.0 1.9 copy.39.refs_6_
  11.9 1.9 copy.40.refs_7_
  13.8 200.0 %shard_map.331 = (bf16[1024,768]{1,0:T(8,128)(2,1)}, f32[1024,768]{1,0:T(8,128)}, bf16[3,768,768]{2,1,0:T(8,128)(2,1)}, f32[8,768]{1,0:T(8,128)}, f32[8,128]{1,0:T(8,128)}) custom-call(s32[2,7]{1,0:T(2,128)} %refs_0_.1, s32[12]{0:T(128)} %refs_1_.1, s32[16]{0:T(128)} %refs_2_.1, f32[9,768]{1,0:T(8,128)} %stack.39.refs_3_, bf16[1024,768]{1,0:T(8,128)(2,1)} %refs_4_.1, ...), custom_call_target="tpu_custom_call" | custom-call | tf_op jit(solution)/shard_map/pallas_call | solution.py:801
  213.8 1.2 slice_bitcast_fusion.4
  214.9 4.6 %bitcast_convert_fusion = (f32[768,768]{1,0:T(8,128)}, f32[768,768]{1,0:T(8,128)}, f32[1,768,768]{2,1,0:T(8,128)S(1)}) fusion(bf16[3,768,768]{2,1,0:T(8,128)(2,1)} %get-tuple-element.26), kind=kLoop, calls=%fused_computation | loop fusion | flops 1769472 | bytes 10616832 | tf_op jit(solution)/shard_map/convert_element_type | solution.py:813
  219.6 0.0 copy-start.2
  219.6 0.0 copy-start.1
  219.6 1.4 slice_bitcast_fusion
  221.0 0.0 copy-start
  221.0 0.0 copy-done.2
  221.0 0.6 fusion
  221.6 0.7 slice_reduce_fusion
  222.2 0.0 copy-done.1
  222.2 1.1 copy.43
  223.4 0.0 copy-done
  223.4 1.7 copy.44
  (2 shorter events, 0.0 us)
Async XLA Ops:
  219.6 1.4 copy-start.2
  219.6 2.7 %copy-start.1 = (bf16[1024,768]{1,0:T(8,128)(2,1)S(1)}, bf16[1024,768]{1,0:T(8,128)(2,1)}, u32[]{:S(2)}) copy-start(bf16[1024,768]{1,0:T(8,128)(2,1)} %get-tuple-element.62) | copy-start | bytes 4718596
  221.0 2.4 %copy-start = (f32[1024,768]{1,0:T(8,128)S(1)}, f32[1024,768]{1,0:T(8,128)}, u32[]{:S(2)}) copy-start(f32[1024,768]{1,0:T(8,128)} %get-tuple-element.64) | copy-start | bytes 9437188

commit v2 on v1

v2 whole, which is shorter than its diff:
```python
import functools
import types

import jax
import jax.numpy as jnp
from jax import lax
from jax.experimental import pallas as pl
from jax.experimental.pallas import tpu as pltpu
from jax.sharding import PartitionSpec as P

HEAD_DIM = 64
MAX_PIECE = 128
NEG_FILL = -1e30
NORM_EPS = 1e-12
UNIT_EPS = 1e-06
SIM_SCALE = 50.0
MESH = pl.DeviceIdType.MESH
F32, BF16, I32 = jnp.float32, jnp.bfloat16, jnp.int32
HIGHEST = lax.Precision.HIGHEST


def nn(a, b):
    return lax.dot_general(a, b, (((1,), (0,)), ((), ())), preferred_element_type=F32)


def nt(a, b):
    return lax.dot_general(a, b, (((1,), (1,)), ((), ())), preferred_element_type=F32)


def tn(a, b):
    return lax.dot_general(a, b, (((0,), (0,)), ((), ())), preferred_element_type=F32)


def iota(shape, axis):
    return lax.broadcasted_iota(I32, shape, axis)


def hi_lo(x):
    hi = x.astype(BF16).astype(F32)
    return hi, x - hi


def layer_kernel(z, names, *refs):
    ns = types.SimpleNamespace(**dict(zip(names, refs)))
    n_dp, R, S, D, L, F, heads = z.n_dp, z.R, z.S, z.D, z.L, z.F, z.heads
    QB, KW = z.QB, z.KW
    n_qb, half = S // QB, QB // 2
    NC = R * n_qb
    CH = D // 128
    dp, mp = lax.axis_index("dp"), lax.axis_index("mp")
    core = mp % 2
    other = 1 - core
    sib = (dp, mp + 1 - 2 * core)
    across = (dp, (mp + 2) % 4)

    bar = pltpu.get_barrier_semaphore()
    for t in (sib, across):
        pl.semaphore_signal(bar, inc=1, device_id=t, device_id_type=MESH)
    for d in range(1, n_dp):
        pl.semaphore_signal(bar, inc=1, device_id=((dp + d) % n_dp, mp), device_id_type=MESH)

    loads = []
    for i, (src, dst) in enumerate((
        (ns.tokens, ns.tokens_v), (ns.wq, ns.wq_v), (ns.wk, ns.wk_v), (ns.wv, ns.wv_v), (ns.wo, ns.wo_v),
        (ns.wu, ns.wu_v), (ns.wd, ns.wd_v), (ns.og, ns.og_v),
    )):
        loads.append(pltpu.make_async_copy(src, dst, ns.in_sem.at[i]))
        loads[-1].start()
    vecs = ns.vecs
    for i, x in enumerate((
        ns.b_query, ns.b_value, ns.output_bias, ns.first_norm_gain, ns.first_norm_bias, ns.b_up, ns.down_bias,
        ns.second_norm_gain, ns.second_norm_bias,
    )):
        n = x.shape[0]
        vecs[i : i + 1, 0:n] = x[...].reshape(1, n)
    pl.semaphore_wait(bar, 1 + n_dp)

    sends = []

    def remote(src, dst, ss, rs, to):
        return pltpu.make_async_remote_copy(
            src_ref=src, dst_ref=dst, send_sem=ss, recv_sem=rs, device_id=to, device_id_type=MESH
        )

    def vec(i, n=None):
        return vecs[i : i + 1, : (n or D)]

    ends = []
    for r in range(R):
        total, row = 0, []
        for p in range(7):
            total = total + ns.lengths[r, p]
            row.append(total)
        ends.append(row)

    def seg_of(position, r):
        seg = jnp.zeros(position.shape, I32)
        for p in range(6):
            seg = seg + jnp.where(position >= ends[r][p], 1, 0)
        return seg

    lane_head = iota((1, L), 1) // HEAD_DIM

    def only_head(x, h):
        return jnp.where(lane_head == h, x, jnp.zeros_like(x))

    in_flight = {}
    unsent = {}

    def finish_send(key):
        if key in unsent:
            sem, copy = unsent.pop(key)
            copy.wait_send()
            del in_flight[sem]

    def begin_send(key, sem, copy):
        if sem in in_flight:
            finish_send(in_flight[sem])
        in_flight[sem] = key
        unsent[key] = (sem, copy)
        copy.start()

    def pair_copy(which, c):
        par = which % 2
        return remote(ns.part.at[par, c, pl.ds(pl.multiple_of(other * half, half), half)], ns.arecv.at[par, c],
                      ns.a_s.at[par], ns.a_r.at[par, c], sib)

    def cross_copy(which, c):
        par = which % 2
        return remote(ns.ysend.at[par, c], ns.yrecv.at[par, c], ns.y_s.at[par, c], ns.y_r.at[par, c], across)

    def send_part(which, c, compute):
        part = ns.part.at[which % 2, c]

        def put(cols, val):
            part[:, cols] = val.astype(BF16)

        if which >= 2:
            finish_send((0, which - 2, c))
        compute(c, put)
        begin_send((0, which, c), (0, which % 2), pair_copy(which, c))

    def send_across(which, c):
        par = which % 2
        pair_copy(which, c).wait_recv()
        if which >= 2:
            finish_send((1, which - 2, c))
        own = pl.ds(pl.multiple_of(core * half, half), half)
        ns.ysend[par, c] = ns.part[par, c, own] + ns.arecv[par, c]
        begin_send((1, which, c), (1, which % 2, c), cross_copy(which, c))

    def y_total(which, c, rows):
        par = which % 2
        return ns.ysend[par, c, rows].astype(F32) + ns.yrecv[par, c, rows].astype(F32)

    def at_chunk(c):
        return slice(c * QB, c * QB + QB)

    def halves(i, c):
        rows = pl.ds(pl.multiple_of(c * QB + core * half, half), half)
        x = (ns.hl, ns.res, ns.d2l, ns.d1l, ns.tg)[i]
        return remote(x.at[rows], x.at[rows], ns.g_s.at[i], ns.g_r.at[G_SLOT[i], c], sib)

    def to_sibling(i, c):
        begin_send((2, i, c), (2, i), halves(i, c))

    TR = z.TR

    def by_rows(fn):
        def body(i, _):
            fn(pl.ds(pl.multiple_of(i * TR, TR), TR), i * TR)
            return 0

        lax.fori_loop(0, half // TR, body, 0, unroll=z.unroll)

    def fold(x):
        return jnp.sum(x.reshape(x.shape[0] // 8, 8, x.shape[1]), axis=0)

    def row_ds(c, start, n):
        return pl.ds(pl.multiple_of(c * QB + core * half + start, n), n)

    def columns(width, step=256):
        return [slice(n, n + step) for n in range(0, width, step)]

    def project(r):
        rows = pl.ds(r * S, S)
        x = ns.tokens_v[rows, :]
        ns.q[rows, :] = ((nt(x, ns.wq_v[...]) + vec(0, L)).astype(BF16) * (HEAD_DIM**-0.5)).astype(BF16)
        ns.k[rows, :] = nt(x, ns.wk_v[...]).astype(BF16)
        ns.v[rows, :] = (nt(x, ns.wv_v[...]) + vec(1, L)).astype(BF16)

    def win(b):
        return min(max(b * QB - MAX_PIECE, 0), S - KW)

    def attend(c):
        r, b = c // n_qb, c % n_qb
        q0, k0 = c * QB, r * S + win(b)
        same = seg_of(iota((QB, 1), 0) + b * QB, r) == seg_of(iota((1, KW), 1) + win(b), r)
        qb = ns.q[q0 : q0 + QB, :]
        kb = ns.k[k0 : k0 + KW, :]
        vb = ns.v[k0 : k0 + KW, :]
        ctx = None
        for h in range(heads):
            s = jnp.where(same, nt(only_head(qb, h), kb), NEG_FILL)
            e = jnp.exp(s - jnp.max(s, axis=-1, keepdims=True))
            p = (e * (1.0 / jnp.sum(e, axis=-1, keepdims=True))).astype(BF16)
            ns.probs[c * heads + h] = p
            o = nn(p, only_head(vb, h))
            ctx = o if ctx is None else ctx + o
        ns.ctx[q0 : q0 + QB, :] = ctx.astype(BF16)

    def attn_out(c, put):
        x = ns.ctx[at_chunk(c), :]
        for w in columns(D):
            put(w, nn(x, ns.wo_v[:, w]))

    def norm(v):
        mean = jnp.mean(v, axis=-1, keepdims=True)
        d = v - mean
        rstd = lax.rsqrt(jnp.mean(d * d, axis=-1, keepdims=True) + NORM_EPS)
        return d * rstd, rstd

    def first_norm(c):
        def body(rows, start):
            mine = row_ds(c, start, TR)
            xh, rstd = norm(ns.tokens_v[mine].astype(F32) + y_total(0, c, rows) + vec(2))
            ns.xhat1[c, rows] = xh
            ns.rstd1[c, rows] = rstd
            h = xh * vec(3) + vec(4)
            ns.hid[c, rows] = h
            ns.hl[mine] = h.astype(BF16)

        by_rows(body)

    def ffn_up(c):
        x = ns.hl[at_chunk(c), :]
        for w in columns(F):
            u = nn(x, ns.wu_v[:, w]) + vecs[5:6, w]
            phi = 0.5 + 0.5 * lax.erf(u * 0.7071067811865476)
            ns.act[at_chunk(c), w] = (u * phi).astype(BF16)
            ns.gp[at_chunk(c), w] = (phi + u * (jnp.exp(-0.5 * (u * u)) * 0.3989422804014327)).astype(BF16)

    def ffn_down(c, put):
        x = ns.act[at_chunk(c), :]
        for w in columns(D):
            put(w, nn(x, ns.wd_v[:, w]))

    def second_norm(c):
        r, b = c // n_qb, c % n_qb

        def body(rows, start):
            xh, rstd = norm(ns.hid[c, rows] + y_total(1, c, rows) + vec(6))
            ns.xhat2[c, rows] = xh
            ns.rstd2[c, rows] = rstd
            res = xh * vec(7) + vec(8)
            low = res.astype(BF16)
            ns.res[row_ds(c, start, TR)] = low
            ns.rest[rows] = (res - low.astype(F32)).astype(BF16)

        by_rows(body)
        piece = iota((8, half), 0)
        seg = seg_of(iota((8, half), 1) + (core * half + b * QB), r)
        member = jnp.where((seg == piece) & (piece < 6), 1.0, 0.0).astype(BF16)
        at = slice(r * 8, r * 8 + 8)
        ns.pool[at, :] += nn(member, ns.res[row_ds(c, 0, half)]) + nn(member, ns.rest[...])

    PR = 16
    n_sent = R * 6

    def per_row(values, axis, shape, fill):
        pos = iota(shape, axis) % PR
        out = jnp.full(shape, fill, I32)
        for s in range(n_sent):
            out = jnp.where(pos == (s // 6) * 8 + s % 6, values[s], out)
        return out

    def slot_onehot(axis):
        shape = (n_dp * 16, CH * PR) if axis == 1 else (CH * PR, n_dp * 16)
        line = (1, CH * PR) if axis == 1 else (CH * PR, 1)
        vals = [ns.send_slot[s] // 2 * 16 + ns.send_slot[s] % 2 for s in range(n_sent)]
        target = per_row(vals, axis if axis == 1 else 0, line, -65536) + iota(line, 1 if axis == 1 else 0) // PR * 2
        return jnp.where(iota(shape, 0 if axis == 1 else 1) == target, 1.0, 0.0).astype(BF16)

    def place_onehot(axis):
        line = (1, n_dp * 16) if axis == 1 else (n_dp * 16, 1)
        shape = (CH * PR, n_dp * 16) if axis == 1 else (n_dp * 16, CH * PR)
        pos = iota(line, axis)
        slot = pos // 16 * 2 + pos % 2
        target = jnp.zeros(line, I32)
        for s in range(2 * n_dp):
            target = jnp.where(slot == s, ns.recv_place[s], target)
        target = target + pos % 16 // 2 * PR
        return jnp.where(iota(shape, 0 if axis == 1 else 1) == target, 1.0, 0.0).astype(BF16)

    def stack(x):
        return jnp.concatenate([x[:, c * 128 : c * 128 + 128] for c in range(CH)], axis=0)

    def unstack(x):
        return jnp.concatenate([x[c * PR : c * PR + PR] for c in range(CH)], axis=1)

    def peers(src, dst, ssem, rsem):
        cs = []
        mine = pl.ds(pl.multiple_of(dp * 16, 16), 16)
        for d in range(1, n_dp):
            t = (dp + d) % n_dp
            c = remote(src.at[pl.ds(pl.multiple_of(t * 16, 16), 16)], dst.at[mine], ssem.at[d], rsem.at[d], (t, mp))
            c.start()
            cs.append(c)
        dst[mine] = src[mine]
        for c in cs:
            c.wait()

    def pairs():
        c = remote(ns.pool, ns.pool_r, ns.pool_sem.at[0], ns.pool_sem.at[1], sib)
        c.start()
        lens = [ns.lengths[s // 6, s % 6] for s in range(n_sent)]
        size = per_row(lens, 0, (PR, 1), 1).astype(F32)
        inv = 1.0 / size
        hot = slot_onehot(1)
        c.wait()
        pooled = (ns.pool[...] + ns.pool_r[...]) * inv
        ns.outg[...] = nn(hot, stack(pooled).astype(BF16)).astype(BF16)
        peers(ns.outg, ns.inc, ns.p_s, ns.p_r.at[0])
        o = unstack(nn(place_onehot(1), ns.inc[...]))
        s = lax.rsqrt(jnp.sum(o * o, axis=-1, keepdims=True) + UNIT_EPS)
        u = o * s
        logits = SIM_SCALE * lax.dot_general(
            u, u, (((1,), (1,)), ((), ())), precision=HIGHEST, preferred_element_type=F32
        )
        i, j = iota((PR, PR), 0), iota((PR, PR), 1)
        live = (i % 2 == 0) & (i < n_sent) & (j % 2 == 1) & (j < n_sent)
        lm = jnp.where(live, logits, NEG_FILL)
        peak = jnp.max(lm, axis=-1, keepdims=True)
        e = jnp.where(live, jnp.exp(lm - peak), 0.0)
        tot = jnp.maximum(jnp.sum(e, axis=-1, keepdims=True), 1e-30)
        partner = live & (j == i + 1)
        loss = peak + jnp.log(tot) - jnp.sum(jnp.where(partner, logits, 0.0), axis=-1, keepdims=True)
        i2, j2 = iota((PR, 128), 0), iota((PR, 128), 1)
        ns.loss_v[...] = jnp.broadcast_to(
            jnp.sum(jnp.where((i2 == 2 * j2) & (i2 < n_sent), loss, 0.0), axis=0, keepdims=True), (8, 128)
        )
        dl = e / tot - jnp.where(partner, 1.0, 0.0)
        du = SIM_SCALE * (
            lax.dot_general(dl, u, (((1,), (0,)), ((), ())), precision=HIGHEST, preferred_element_type=F32)
            + lax.dot_general(dl, u, (((0,), (0,)), ((), ())), precision=HIGHEST, preferred_element_type=F32)
        )
        do = s * (du - u * jnp.sum(u * du, axis=-1, keepdims=True))
        ns.outg2[...] = nn(place_onehot(0), stack(do).astype(BF16)).astype(BF16)
        peers(ns.outg2, ns.inc2, ns.p_s, ns.p_r.at[1])
        ns.dpool[...] = unstack(nn(slot_onehot(0), ns.inc2[...])) * inv

    def norm_back(dx, xh, rstd):
        return rstd * (
            dx - jnp.mean(dx, axis=-1, keepdims=True) - xh * jnp.mean(dx * xh, axis=-1, keepdims=True)
        )

    def second_norm_back(c):
        r, b = c // n_qb, c % n_qb
        hi, lo = hi_lo(ns.dpool[r * 8 : r * 8 + 8, :])
        lane = iota((half, 16), 1) % 8
        seg = seg_of(iota((half, 1), 0) + (core * half + b * QB), r)
        member = jnp.where((seg == lane) & (lane < 6), 1.0, 0.0).astype(BF16)
        ns.dtok[...] = nn(member, jnp.concatenate([hi, lo], axis=0).astype(BF16))

        def body(rows, start):
            mine = row_ds(c, start, TR)
            d = ns.og_v[mine].astype(F32) + ns.dtok[rows]
            xh = ns.xhat2[c, rows]
            ns.acc[4] += fold(d * xh)
            ns.acc[5] += fold(d)
            d2 = norm_back(d * vec(7), xh, ns.rstd2[c, rows])
            ns.acc[3] += fold(d2)
            ns.d2[c, rows] = d2
            ns.d2l[mine] = d2.astype(BF16)

        by_rows(body)

    def ffn_back(c):
        rows = at_chunk(c)
        x = ns.d2l[rows, :]
        for w in columns(F):
            da = nt(x, ns.wd_v[w, :]).astype(BF16)
            du = (da.astype(F32) * ns.gp[rows, w].astype(F32)).astype(BF16)
            ns.dup[rows, w] = du
            ns.acc[6, :, w] += fold(du.astype(F32))

    def ffn_back_out(c, put):
        x = ns.dup[at_chunk(c), :]
        for w in columns(D):
            put(w, nt(x, ns.wu_v[w, :]))

    def down_weights(n):
        for w in columns(F)[n : n + 1]:
            grad[0, w, :] = tn(ns.act[:, w], ns.d2l[...]).astype(BF16)

    def up_weights(n):
        for w in columns(D)[n : n + 1]:
            grad[1, w, :] = tn(ns.hl[:, w], ns.dup[...]).astype(BF16)

    def first_norm_back(c):
        def body(rows, start):
            mine = row_ds(c, start, TR)
            d = ns.d2[c, rows] + y_total(2, c, rows)
            xh = ns.xhat1[c, rows]
            ns.acc[1] += fold(d * xh)
            ns.acc[2] += fold(d)
            d1 = norm_back(d * vec(3), xh, ns.rstd1[c, rows])
            ns.acc[0] += fold(d1)
            ns.d1[c, rows] = d1
            ns.d1l[mine] = d1.astype(BF16)

        by_rows(body)

    def attend_back(c):
        r, b = c // n_qb, c % n_qb
        q0, k0 = c * QB, r * S + win(b)
        cb = nt(ns.d1l[at_chunk(c), :], ns.wo_v[...]).astype(BF16)
        qb = ns.q[q0 : q0 + QB, :]
        kb = ns.k[k0 : k0 + KW, :]
        vb = ns.v[k0 : k0 + KW, :]
        dq = dk = dv = None
        for h in range(heads):
            p = ns.probs[c * heads + h]
            dp_ = nt(cb, only_head(vb, h))
            pf = p.astype(F32)
            delta = jnp.sum(pf * dp_, axis=-1, keepdims=True)
            ds = (pf * (dp_ - delta)).astype(BF16)
            t, u, w = nn(ds, only_head(kb, h)), tn(ds, only_head(qb, h)), tn(p, only_head(cb, h))
            dq, dk, dv = (t, u, w) if dq is None else (dq + t, dk + u, dv + w)
        dq = (dq * (HEAD_DIM**-0.5)).astype(BF16)
        ns.dq[q0 : q0 + QB, :] = dq
        ns.acc[7, :, :L] += fold(dq.astype(F32))
        at = slice(win(b), win(b) + KW)
        if b == 0:
            ns.dk_acc[...] = jnp.zeros((S, L), F32)
            ns.dv_acc[...] = jnp.zeros((S, L), F32)
        ns.dk_acc[at, :] += dk
        ns.dv_acc[at, :] += dv
        if b == n_qb - 1:
            rows = slice(r * S, r * S + S)
            ns.dk[rows, :] = ns.dk_acc[...].astype(BF16)
            dvr = ns.dv_acc[...].astype(BF16)
            ns.dv[rows, :] = dvr
            ns.acc[8, :, :L] += fold(dvr.astype(F32))

    def attend_back_out(c, put):
        at = at_chunk(c)
        for w in columns(D):
            put(
                w,
                nn(ns.dq[at, :], ns.wq_v[:, w])
                + nn(ns.dk[at, :], ns.wk_v[:, w])
                + nn(ns.dv[at, :], ns.wv_v[:, w]),
            )

    def attend_weights():
        for i, x in enumerate((ns.dq, ns.dk, ns.dv)):
            grad[2, i * L : i * L + L, :] = tn(x[...], ns.tokens_v[...]).astype(BF16)
        grad[2, 3 * L : 4 * L, :] = tn(ns.ctx[...], ns.d1l[...]).astype(BF16)

    def finish(c):
        def body(rows, start):
            ns.tg[row_ds(c, start, TR)] = ns.d1[c, rows] + y_total(3, c, rows)

        by_rows(body)

    xi, zi = dp % 2, dp // 2
    nz = n_dp // 2
    in_kernel = z.in_kernel
    outer = (zi == 0) | (zi == nz - 1)
    inner = (zi != 0) & (zi != nz - 1)
    xp = (dp + 1 - 2 * xi, mp)
    zp = (dp + 2 - 4 * (zi % 2), mp)
    zq = ((dp + 2 * (3 - 2 * zi)) % n_dp if in_kernel else dp, mp)
    ii = zi // 2
    grad, gsum = ns.grad, ns.gsum

    def when(condition, fn):
        return lambda: pl.when(condition)(fn)

    def add_into(dst, dst_at, a_at, b_at, n):
        step = 48 if n % 48 == 0 else 32 if n % 32 == 0 else 16

        def body(i, _):
            o = i * step
            x = grad[a_at[0], pl.ds(pl.multiple_of(a_at[1] + o, 16), step), :]
            y = ns.rx[pl.ds(pl.multiple_of(b_at + o, 16), step), :]
            dst[dst_at[0], pl.ds(pl.multiple_of(dst_at[1] + o, 16), step), :] = x + y
            return 0

        lax.fori_loop(0, n // step, body, 0)

    def x_job(slot, j, r0, n):
        h = n // 2
        mine = pl.multiple_of(r0 + xi * h, 16)
        yours = pl.multiple_of(r0 + (1 - xi) * h, 16)
        own, theirs = pl.ds(mine, h), pl.ds(yours, h)
        s = lambda k: ns.d_s.at[z.slots[slot], k]
        q = lambda k: ns.d_r.at[slot, k]
        b0 = z.rx_at[slot]
        buf = lambda k: ns.rx.at[pl.ds(b0 + k * h, h)]
        x1 = remote(grad.at[j, theirs], buf(0), s(0), q(0), xp)
        z1 = remote(grad.at[j, own], buf(1), s(0), q(1), zp)
        z2 = remote(grad.at[j, own], buf(2), s(0), q(2), zq)
        z3 = remote(gsum.at[j, own], gsum.at[j, own], s(1), q(1), zp)
        x2 = remote(gsum.at[j, own], gsum.at[j, own], s(0), q(3), xp)

        def s1o():
            x1.wait()
            add_into(grad, (j, mine), (j, mine), b0, h)
            z1.start()

        def s1i():
            x1.wait()
            add_into(grad, (j, mine), (j, mine), b0, h)

        def s2():
            z1.wait_recv()
            add_into(grad, (j, mine), (j, mine), b0 + h, h)
            z2.start()

        def s3():
            z2.wait()
            add_into(gsum, (j, mine), (j, mine), b0 + 2 * h, h)
            z3.start()
            x2.start()

        def s4():
            z3.wait_recv()
            z1.wait_send()
            x2.start()

        def end():
            x2.wait_send()
            pl.when(inner)(z3.wait_send)

        steps = {0: x1.start, 1: when(outer, s1o), 8: when(inner, s1i), 2: when(inner, s2), 3: when(inner, s3),
                 4: when(outer, s4), 5: x2.wait_recv}
        return steps, end

    def z_job(slot, j, r0, n):
        h = n // 2
        mine = pl.multiple_of(r0 + ii * h, 16)
        yours = pl.multiple_of(r0 + (1 - ii) * h, 16)
        own, theirs, whole = pl.ds(mine, h), pl.ds(yours, h), pl.ds(r0, n)
        s = lambda k: ns.d_s.at[z.slots[slot], k]
        q = lambda k: ns.d_r.at[slot, k]
        b0 = z.rx_at[slot]
        buf = lambda k: ns.rx.at[pl.ds(b0 + k * h, h)]
        z1 = remote(grad.at[j, whole], ns.rx.at[pl.ds(b0 + n, n)], s(0), q(0), zp)
        z2 = remote(grad.at[j, theirs], buf(0), s(0), q(1), zq)
        x = remote(grad.at[j, own], buf(1), s(1), q(2), xp)
        z2b = remote(gsum.at[j, own], gsum.at[j, own], s(0), q(3), zq)
        z3a = remote(gsum.at[j, own], gsum.at[j, own], s(1), q(1), zp)
        z3b = remote(gsum.at[j, theirs], gsum.at[j, theirs], s(0), q(2), zp)

        def s1():
            z1.wait_recv()
            add_into(grad, (j, r0), (j, r0), b0 + n, n)
            z2.start()

        def s2():
            z2.wait_recv()
            add_into(grad, (j, mine), (j, mine), b0, h)
            x.start()

        def s3():
            x.wait()
            z2.wait_send()
            add_into(gsum, (j, mine), (j, mine), b0 + h, h)
            z2b.start()
            z3a.start()

        def s4():
            z2b.wait()
            z3b.start()

        def s5():
            z3a.wait_recv()
            z3b.wait_recv()

        def end():
            pl.when(outer)(z1.wait_send)

            @pl.when(inner)
            def _():
                z3a.wait_send()
                z3b.wait_send()

        steps = {0: when(outer, z1.start), 1: when(inner, s1), 2: when(inner, s2), 3: when(inner, s3),
                 4: when(inner, s4), 5: when(outer, s5)}
        return steps, end

    def q_job(slot, j, r0, n):
        h, f = n // 2, n // 4
        mine = pl.multiple_of(r0 + ii * h, 16)
        yours = pl.multiple_of(r0 + (1 - ii) * h, 16)
        own, theirs, whole = pl.ds(mine, h), pl.ds(yours, h), pl.ds(r0, n)
        back_a = pl.ds(pl.multiple_of(mine + xi * f, 16), f)
        back_b = pl.ds(pl.multiple_of(yours + xi * f, 16), f)
        s = lambda k: ns.d_s.at[z.slots[slot], k]
        q = lambda k: ns.d_r.at[slot, k]
        b0 = z.rx_at[slot]
        buf = lambda k: ns.rx.at[pl.ds(b0 + k * h, h)]
        z1 = remote(grad.at[j, whole], ns.rx.at[pl.ds(b0 + n, n)], s(0), q(0), zp)
        z2 = remote(grad.at[j, theirs], buf(0), s(0), q(1), zq)
        x = remote(grad.at[j, own], buf(1), s(1), q(2), xp)
        z2b = remote(gsum.at[j, own], gsum.at[j, own], s(0), q(3), zq)
        z3a = remote(gsum.at[j, back_a], gsum.at[j, back_a], s(1), q(0), zp)
        z3b = remote(gsum.at[j, back_b], gsum.at[j, back_b], s(0), q(1), zp)
        xa = remote(gsum.at[j, back_a], gsum.at[j, back_a], s(0), q(2), xp)
        xb = remote(gsum.at[j, back_b], gsum.at[j, back_b], s(1), q(3), xp)

        def s1():
            z1.wait_recv()
            add_into(grad, (j, r0), (j, r0), b0 + n, n)
            z2.start()

        def s2():
            z2.wait_recv()
            add_into(grad, (j, mine), (j, mine), b0, h)
            x.start()

        def s3():
            x.wait()
            z2.wait_send()
            add_into(gsum, (j, mine), (j, mine), b0 + h, h)
            z2b.start()
            z3a.start()

        def s4():
            z2b.wait()
            z3b.start()

        def s5():
            z3a.wait_recv()
            z1.wait_send()
            xa.start()
            z3b.wait_recv()
            xb.start()

        def s6():
            xa.wait_recv()
            xb.wait_recv()

        def end():
            @pl.when(outer)
            def _():
                xa.wait_send()
                xb.wait_send()

            @pl.when(inner)
            def _():
                z3a.wait_send()
                z3b.wait_send()

        steps = {0: when(outer, z1.start), 1: when(inner, s1), 2: when(inner, s2), 3: when(inner, s3),
                 4: when(inner, s4), 5: when(outer, s5), 6: when(outer, s6)}
        return steps, end

    def u_job(slot, j, r0, n):
        near = pl.multiple_of(r0 + ii * n, 16)
        far = pl.multiple_of(r0 + (1 - ii) * n, 16)
        near_d, far_d = pl.ds(near, n), pl.ds(far, n)
        s = lambda k: ns.d_s.at[z.slots[slot], k]
        q = lambda k: ns.d_r.at[slot, k]
        b0 = z.rx_at[slot]
        buf = lambda k: ns.rx.at[pl.ds(b0 + k * n, n)]
        za = remote(grad.at[j, far_d], buf(0), s(0), q(0), zp)
        ma = remote(grad.at[j, far_d], buf(1), s(0), q(1), zq)
        zb = remote(grad.at[j, near_d], buf(0), s(1), q(0), zp)
        xa = remote(grad.at[j, near_d], buf(1), s(1), q(1), xp)
        zc = remote(gsum.at[j, near_d], gsum.at[j, near_d], s(0), q(2), zp)
        mb = remote(gsum.at[j, near_d], gsum.at[j, near_d], s(0), q(3), zq)
        zd = remote(gsum.at[j, far_d], gsum.at[j, far_d], s(1), q(2), zp)

        def s1():
            za.wait_recv()
            add_into(grad, (j, far), (j, far), b0, n)
            ma.start()

        def s2():
            ma.wait_recv()
            add_into(grad, (j, near), (j, near), b0 + n, n)
            zb.start()

        def s3():
            zb.wait_recv()
            add_into(grad, (j, near), (j, near), b0, n)
            xa.start()

        def s4():
            xa.wait_recv()
            za.wait_send()
            add_into(gsum, (j, near), (j, near), b0 + n, n)
            zc.start()

        def s5():
            zc.wait_recv()
            ma.wait_send()
            mb.start()

        def s6():
            mb.wait_recv()
            zb.wait_send()
            zd.start()

        def end():
            @pl.when(outer)
            def _():
                xa.wait_send()
                zc.wait_send()

            @pl.when(inner)
            def _():
                mb.wait_send()
                zd.wait_send()

        steps = {0: when(outer, za.start), 1: when(inner, s1), 2: when(inner, s2), 3: when(outer, s3),
                 4: when(outer, s4), 5: when(inner, s5), 6: when(inner, s6), 7: when(outer, zd.wait_recv)}
        return steps, end

    def vector_job():
        vg, vr = ns.vg, ns.vr
        s = lambda k: ns.v_s.at[k]
        q = lambda k: ns.v_r.at[k]
        z1 = remote(vg, vr.at[0], s(0), q(0), zp)
        z2 = remote(vg, vr.at[1], s(0), q(1), zq)
        x = remote(vg, vr.at[2], s(1), q(2), xp)
        z3 = remote(ns.vt, ns.vt, s(0), q(0), zp)

        def c1():
            z1.wait_recv()
            vg[...] = vg[...] + vr[0]
            z2.start()

        def c2():
            z2.wait_recv()
            z2.wait_send()
            vg[...] = vg[...] + vr[1]
            x.start()

        def c3():
            x.wait_recv()
            ns.vt[...] = vg[...] + vr[2]
            z3.start()

        def end():
            pl.when(outer)(z1.wait_send)

            @pl.when(inner)
            def _():
                x.wait_send()
                z3.wait_send()

        steps = {0: when(outer, z1.start), 1: when(inner, c1), 2: when(inner, c2), 3: when(inner, c3),
                 4: when(outer, z3.wait_recv)}
        return steps, end

    tasks, ends_of = {}, {}
    if in_kernel:
        for i, (kind, j, r0, n) in enumerate(z.jobs):
            steps, end = (x_job, z_job, q_job, u_job)[kind](i, j, r0, n)
            tasks.update({JOB + i * 10 + k: f for k, f in steps.items()})
            ends_of[i] = end
        steps, end = vector_job()
        tasks.update({VECTOR + k: f for k, f in steps.items()})
        ends_of[-1] = end

    waited = set()

    def once(key, fn):
        if key not in waited:
            waited.add(key)
            fn()

    def load(*keys):
        for k in keys:
            once((9, k), loads[k].wait)

    def come(i, c):
        once((i, c), halves(i, c).wait_recv)

    ns.pool[...] = jnp.zeros((PR, D), F32)
    ns.acc[...] = jnp.zeros(ns.acc.shape, F32)

    def run_project(r):
        load(0, 1, 2, 3)
        project(r)

    def run_out(c):
        load(4)
        send_part(0, c, attn_out)

    def run_norm(c):
        cross_copy(0, c).wait_recv()
        first_norm(c)
        to_sibling(0, c)

    def run_up(c):
        load(5)
        come(0, c)
        ffn_up(c)

    def run_down(c):
        load(6)
        send_part(1, c, ffn_down)

    def run_second(c):
        cross_copy(1, c).wait_recv()
        second_norm(c)
        to_sibling(1, c)

    forward = (run_project, attend, run_out, functools.partial(send_across, 0), run_norm, run_up, run_down,
               functools.partial(send_across, 1), run_second)
    if NC == 4:
        plan = FORWARD
    else:
        plan = [r for r in range(R)]
        for group in ((1, 2, 3), (4, 5, 6, 7), (8,)):
            plan += [10 * k + c for c in range(NC) for k in group]
    for k in plan:
        forward[k // 10](k % 10)
    load(7)
    pairs()

    def run_second_back(c):
        second_norm_back(c)
        to_sibling(2, c)

    def run_down_weights(n):
        for i in range(NC):
            come(2, i)
        down_weights(n)

    def run_ffn_back(c):
        come(2, c)
        ffn_back(c)

    def run_first_back(c):
        cross_copy(2, c).wait_recv()
        first_norm_back(c)
        to_sibling(3, c)

    def run_attend_back(c):
        come(3, c)
        attend_back(c)

    def run_finish(c):
        cross_copy(3, c).wait_recv()
        finish(c)
        to_sibling(4, c)

    def run_results(_):
        for i in range(NC):
            come(1, i)

    def vector_copy():
        return remote(ns.vmine, ns.vsib, ns.pool_sem.at[2], ns.pool_sem.at[3], sib)

    def run_vectors(_):
        for i in range(7):
            ns.vmine[i : i + 1, :] = jnp.sum(ns.acc[i], axis=0, keepdims=True)
        ns.vmine[7:8, :] = jnp.zeros((1, D), F32)
        ns.vmine[7:8, 0:L] = jnp.sum(ns.acc[7], axis=0, keepdims=True)[:, :L]
        ns.vmine[7:8, 256 : 256 + L] = jnp.sum(ns.acc[8], axis=0, keepdims=True)[:, :L]
        vector_copy().start()

    def run_vectors_sum(_):
        vector_copy().wait()
        v = ns.vmine[...] + jnp.where(iota((8, D), 0) < 6, ns.vsib[...], 0.0)
        ns.vg[...] = jnp.concatenate([v[:, : D // 2], v[:, D // 2 :]], axis=0).astype(BF16)

    backward = (
        run_second_back, run_down_weights, run_ffn_back, lambda c: send_part(2, c, ffn_back_out),
        functools.partial(send_across, 2), up_weights, run_first_back, run_attend_back,
        lambda c: send_part(3, c, attend_back_out), functools.partial(send_across, 3), lambda _: attend_weights(),
        run_finish, functools.partial(come, 4), run_results, run_vectors, run_vectors_sum,
    )
    for k in z.order:
        if k in tasks:
            if k in z.free_before:
                ends_of.pop(z.free_before[k])()
            tasks[k]()
        elif k < VECTOR:
            backward[k // 10](k % 10)
    for end in ends_of.values():
        end()
    if not in_kernel:
        gsum[...] = grad[...]
        ns.vt[...] = ns.vg[...]
    for key in list(unsent):
        finish_send(key)
    for c in sends:
        c.wait_send()


def unpack_kernel(z, g, res_i, tg_i, vec, loss_i, gd, gu, res, tg, gq, gk, gv, go, *more):
    L, R, D = z.L, z.R, z.D
    ones, (bq, bv, loss, wide, sem) = more[:7], more[7:]
    stores = []

    def store(src, dst):
        stores.append(pltpu.make_async_copy(src, dst, sem.at[len(stores)]))
        stores[-1].start()

    rows = tg.shape[0] // 4
    for i in range(4):
        at = pl.ds(i * rows, rows)
        store(tg_i.at[at], tg.at[at])
    for m in range(3):
        for i, r in enumerate(range(0, D, L)):
            at = pl.ds(r, L)
            wide[m, at] = g[m, at].astype(F32)
            store(wide.at[m, at], (gq, gk, gv, go)[i] if m == 2 else (gd, gu)[m].at[at])
    for i in range(2):
        at = pl.ds(2 * i * rows, 2 * rows)
        store(res_i.at[at], res.at[at])
    v = vec[...].astype(F32)
    v = jnp.concatenate([v[:8], v[8:]], axis=1)
    for n, one in enumerate(ones):
        one[...] = v[n, :]
    bq[...] = v[7, 0:L]
    bv[...] = v[7, 256 : 256 + L]
    loss[...] = loss_i[0, 0 : R * 3]
    for c in stores:
        c.wait()


FORWARD = (
    0, 10, 20, 1, 30, 11, 21, 12, 31, 22, 13, 32, 23, 33, 40, 50, 60, 41, 70, 51, 61, 42, 71, 52, 62, 43, 72,
    53, 63, 73, 80, 81, 82, 83,
)
JOBS = (
    (0, 0, 32), (1, 0, 32), (3, 0, 80), (0, 0, 32), (0, 0, 96), (1, 0, 64), (0, 0, 96), (0, 0, 96), (1, 0, 64),
    (0, 0, 96), (3, 1, 80), (0, 1, 96), (1, 1, 96), (0, 1, 96), (0, 1, 96), (0, 1, 96), (1, 1, 64), (0, 1, 64),
    (0, 2, 96), (1, 2, 64), (0, 2, 96), (1, 2, 64), (0, 2, 96), (1, 2, 64), (0, 2, 96), (1, 2, 64), (0, 2, 64),
    (1, 2, 64),
)
VECTOR, JOB = 200, 1000
ORDER = (
    0, 1, 2, 3, 21, 10, 1010, 1000, 11, 1040, 1030, 1020, 12, 1070, 22, 1050, 31, 23, 20, 1080, 1060, 30, 1048,
    1011, 50, 51, 1110, 1021, 41, 1012, 1100, 1051, 40, 1013, 1130, 32, 1078, 1120, 52, 1081, 1068, 1041, 1071,
    42, 1052, 1022, 61, 1101, 1170, 1160, 1140, 1001, 33, 1053, 1121, 1082, 1061, 1178, 1014, 1141, 1150, 60,
    1102, 1042, 43, 1031, 70, 1072, 1090, 1138, 1054, 71, 1122, 1023, 1083, 1161, 1148, 1008, 1043, 1073, 1131,
    1062, 62, 1151, 1002, 1103, 80, 1091, 63, 1142, 1098, 1158, 1123, 1084, 72, 1162, 1132, 1063, 1118, 1024,
    73, 140, 1003, 90, 1143, 1152, 100, 82, 1190, 1104, 1092, 1111, 1124, 1163, 81, 1133, 150, 92, 1180, 1210,
    1220, 1025, 1240, 1004, 1074, 1144, 1191, 91, 1250, 1153, 83, 1093, 1015, 1038, 1105, 1055, 1026, 1164,
    130, 1171, 1145, 1032, 1260, 1211, 93, 1192, 200, 1112, 1154, 1181, 1064, 1200, 1106, 1075, 1033, 1230,
    1188, 1228, 110, 1270, 1085, 1251, 1134, 201, 1172, 1212, 1193, 1221, 1034, 1113, 1261, 120, 1044, 1182,
    1231, 112, 1201, 1173, 1213, 1174, 111, 1114, 1252, 1005, 1094, 121, 1271, 1194, 202, 1248, 1107, 1183,
    1268, 1035, 1241, 1222, 1184, 1095, 1224, 204, 1065, 1214, 1027, 1215, 1232, 1125, 1253, 1208, 1202, 203,
    1135, 1204, 113, 1272, 1264, 1262, 1244, 1223, 1185, 1242, 1233, 1155, 1115, 1175, 1255, 1203, 1045, 1263,
    123, 122, 1243, 1225, 1165, 1205, 1273, 1265, 1195, 1254, 1245, 1234, 1235, 1274, 1275,
)
G_SLOT = (0, 1, 0, 0, 2)
VMEM1 = 54 * 2**20


def send_slots(order, n_jobs):
    steps = [(n, k, (k - JOB) // 10) for n, k in enumerate(order) if k >= JOB]
    last = {i: n for n, _, i in steps}
    slots, free_before, done, used = {}, {}, [], 0
    for n, k, i in steps:
        if i not in slots:
            if done:
                old = done.pop(0)
                slots[i], free_before[k] = slots[old], old
            else:
                slots[i], used = used, used + 1
        if last[i] == n:
            done.append(i)
    return slots, free_before, used


def default_order(chunks):
    out = []
    for group in ((0,), (2, 3, 4)):
        out += [10 * k + c for c in range(chunks) for k in group]
    out += [130, 10, 11, 12, 50, 51, 52]
    for group in ((6,), (7,), (8, 9), (11, 12)):
        out += [10 * k + c for c in range(chunks) for k in group]
    return out + [100, 140, 150]


def on_device(n_dp, tokens, lengths, send_slot, recv_place, w_query, b_query, w_key, w_value, b_value, w_out,
              output_bias, first_norm_gain, first_norm_bias, w_up, b_up, w_down, down_bias, second_norm_gain,
              second_norm_bias, out_grad):
    T, D = tokens.shape
    R, L, F = lengths.shape[0], w_query.shape[1], w_up.shape[1]
    S, heads = T // R, L // HEAD_DIM
    QB = 256 if S % 256 == 0 else S
    n_qb, half = S // QB, QB // 2
    KW = min(QB + (MAX_PIECE if n_qb <= 2 else 2 * MAX_PIECE), S)
    NC = R * n_qb
    jobs, rx_at, rx_rows, at = [], [], 0, [0, 0, 0]
    for kind, j, n in JOBS:
        jobs.append((kind, j, at[j], n))
        rx_at.append(rx_rows)
        at[j] += 2 * n if kind == 3 else n
        rx_rows += n // 2 * 3 if kind == 0 else 2 * n
    n_jobs = len(jobs)
    slots, free_before, n_slots = send_slots(ORDER, n_jobs)
    order = ORDER if NC == 4 else default_order(NC)
    in_kernel = n_dp == 8 and at == [D, D, D] and NC == 4
    z = types.SimpleNamespace(n_dp=n_dp, R=R, S=S, D=D, L=L, F=F, heads=heads, in_kernel=in_kernel, QB=QB, KW=KW, TR=32,
                              unroll=4, jobs=jobs, rx_at=rx_at, order=order, slots=slots, free_before=free_before)
    ins = dict(lengths=lengths, send_slot=send_slot, recv_place=recv_place, b_query=b_query, b_value=b_value,
               output_bias=output_bias, first_norm_gain=first_norm_gain, first_norm_bias=first_norm_bias, b_up=b_up,
               down_bias=down_bias, second_norm_gain=second_norm_gain, second_norm_bias=second_norm_bias,
               tokens=tokens, wq=w_query.T, wk=w_key.T, wv=w_value.T, wo=w_out, wu=w_up, wd=w_down, og=out_grad)
    any_, vmem, smem = (pl.BlockSpec(memory_space=m) for m in (pl.ANY, pltpu.VMEM, pltpu.SMEM))
    in_specs = [smem] * 3 + [vmem] * 9 + [any_] * 8
    outs = dict(
        res=((T, D), BF16), tg=((T, D), F32), gsum=((3, D, D), BF16), vt=((16, D // 2), BF16), loss_v=((8, 128), F32)
    )
    V = pltpu.VMEM
    dma = pltpu.SemaphoreType.DMA
    scratch = dict(
        tokens_v=V((T, D), BF16), og_v=V((T, D), BF16), wq_v=V((L, D), BF16), wk_v=V((L, D), BF16),
        wv_v=V((L, D), BF16), wo_v=V((L, D), BF16), wu_v=V((D, F), BF16), wd_v=V((F, D), BF16), vecs=V((9, D), F32),
        q=V((T, L), BF16), k=V((T, L), BF16), v=V((T, L), BF16), ctx=V((T, L), BF16),
        dq=V((T, L), BF16), dk=V((T, L), BF16), dv=V((T, L), BF16), dk_acc=V((S, L), F32), dv_acc=V((S, L), F32),
        probs=V((NC * heads, QB, KW), BF16),
        xhat1=V((NC, half, D), F32), xhat2=V((NC, half, D), F32), hid=V((NC, half, D), F32), d2=V((NC, half, D), F32),
        d1=V((NC, half, D), F32), rstd1=V((NC, half, 1), F32), rstd2=V((NC, half, 1), F32),
        rest=V((half, D), BF16), dtok=V((half, D), F32),
        hl=V((T, D), BF16), act=V((T, F), BF16), gp=V((T, F), BF16), d2l=V((T, D), BF16), dup=V((T, F), BF16),
        d1l=V((T, D), BF16),
        part=V((2, NC, QB, D), BF16), arecv=V((2, NC, half, D), BF16),
        ysend=V((2, NC, half, D), BF16), yrecv=V((2, NC, half, D), BF16),
        pool=V((16, D), F32), pool_r=V((16, D), F32), dpool=V((16, D), F32), acc=V((9, 8, D), F32),
        outg=V((n_dp * 16, 128), BF16), inc=V((n_dp * 16, 128), BF16), outg2=V((n_dp * 16, 128), BF16),
        inc2=V((n_dp * 16, 128), BF16),
        vmine=V((8, D), F32), vsib=V((8, D), F32), vg=V((16, D // 2), BF16), vr=V((3, 16, D // 2), BF16),
        grad=V((3, D, D), BF16), rx=V((rx_rows, D), BF16),
        in_sem=dma((8,)), a_s=dma((2,)), a_r=dma((2, NC)), y_s=dma((2, NC)), y_r=dma((2, NC)),
        g_s=dma((5,)), g_r=dma((3, NC)), pool_sem=dma((4,)), p_s=dma((n_dp,)), p_r=dma((2, n_dp)),
        v_s=dma((2,)), v_r=dma((3,)), d_s=dma((n_slots, 2)), d_r=dma((n_jobs, 4)),
    )
    names = tuple(ins) + tuple(outs) + tuple(scratch)
    res, tg, grads, vec, loss = pl.pallas_call(
        functools.partial(layer_kernel, z, names),
        out_shape=[V(*s) for s in outs.values()],
        in_specs=in_specs,
        out_specs=[vmem] * 5,
        scratch_shapes=list(scratch.values()),
        compiler_params=pltpu.CompilerParams(
            collective_id=0, has_side_effects=True, vmem_limit_bytes=VMEM1
        ),
    )(*ins.values())
    if not z.in_kernel:
        grads, vec = lax.psum((grads, vec), "dp")
    un_outs = [((F, D), F32), ((D, F), F32), ((T, D), BF16), ((T, D), F32)] + [((L, D), F32)] * 4
    n_big = len(un_outs)
    un_outs += [((D,), F32)] * 7 + [((L,), F32)] * 2 + [((R * 3,), F32)]
    o = pl.pallas_call(
        functools.partial(unpack_kernel, z),
        out_shape=[jax.ShapeDtypeStruct(*s) for s in un_outs],
        in_specs=[vmem] * 5,
        out_specs=[any_] * n_big + [vmem] * (len(un_outs) - n_big),
        scratch_shapes=[V((3, D, D), F32), dma((6 + 3 * (D // L),))],
        compiler_params=pltpu.CompilerParams(vmem_limit_bytes=24 * 2**20),
    )(grads, res, tg, vec, loss)
    gd, gu, res, tg, gq, gk, gv, go, v0, v1, v2, v3, v4, v5, v6, bq, bv, loss = o
    return res, loss, tg, gq.T, bq, gk.T, gv.T, bv, go, v0, v1, v2, gu, v6, gd, v3, v4, v5


def solution(mesh):
    rows, flat, cut = P("dp", None), P("dp"), P("mp")
    across, down = P(None, "mp"), P("mp", None)
    return jax.shard_map(
        functools.partial(on_device, mesh.shape["dp"]),
        mesh=mesh,
        in_specs=(rows, rows, flat, flat, across, cut, across, across, cut, down, P(), P(), P(), across, cut, down,
                  P(), P(), P(), rows),
        out_specs=(rows, flat, rows, across, cut, across, across, cut, down, P(), P(), P(), across, cut, down, P(),
                   P(), P()),
        check_vma=False,
    )
```

time: 226 us -> 141 us (0.62)
  Pallas kernels: 200 us -> 140 us
  local copies, waits for them, and re-layouts: 19.8 us -> 0 us
  other arithmetic: 4.62 us -> 0 us
    pallas_call x1 -> x2, Pallas kernels: 200 us -> 140 us  [the longest x1 135 us: on_device(): pl.pallas_call(functools.partial(layer_kernel, z, names), out_shape=[V(*s...]
    unnamed x11 -> x0, local copies, waits for them, and re-layouts: 8.45 us -> none
    another operation x10 -> x0, local copies, waits for them, and re-layouts: 6.1 us -> none  [on_device(): jnp.stack([widen(b_query), widen(b_value), output_bias, first_norm_gain,...]
    convert_element_type x1 -> x0, other arithmetic: 4.62 us -> none  [on_device(): grads[0].astype(F32)]
    slice x3 -> x0, local copies, waits for them, and re-layouts: 2.66 us -> none  [the longest x1 1.44 us: on_device(): ga[3 * L:]]
where the time goes in v2:
time: 141 us
  Pallas kernels  140 us (99%)
    pallas_call x1, Pallas kernels, on_device(): pl.pallas_call(functools.partial(layer_kernel, z, names), out_shape=[V(*s...  135 us
    pallas_call x1, Pallas kernels, on_device(): pl.pallas_call(functools.partial(unpack_kernel, z), out_shape=[jax.ShapeD...  5.09 us

profile of v2, /device:TPU:0, one launch (start us, length us, event | category | flops | bytes accessed | tf_op | source)
XLA Modules:
  0.0 140.8 jit_solution(13169249949576653882)
XLA Ops:
  0.7 134.9 %shard_map.331 = (bf16[1024,768]{1,0:T(8,128)(2,1)S(1)}, f32[1024,768]{1,0:T(8,128)S(1)}, bf16[3,768,768]{2,1,0:T(8,128)(2,1)S(1)}, bf16[16,384]{1,0:T(8,128)(2,1)S(1)}, f32[8,128]{1,0:T(8,128)S(1)}) custom-call(s32[2,7]{1,0:T(2,128)} %refs_0_.1, s32[12]{0:T(128)} %refs_1_.1, s32[16]{0:T(128)} %refs_2_.1, f32[192]{0:T(256)} %refs_3_.1, f32[192]{0:T(256)} %refs_4_.1, ...), custom_call_target="tpu_custom_call" | custom-call | tf_op jit(solution)/shard_map/pallas_call | solution.py:1042
  135.6 5.1 %shard_map.332 = (f32[768,768]{1,0:T(8,128)}, f32[768,768]{1,0:T(8,128)}, bf16[1024,768]{1,0:T(8,128)(2,1)}, f32[1024,768]{1,0:T(8,128)}, f32[192,768]{1,0:T(8,1...) custom-call(bf16[3,768,768]{2,1,0:T(8,128)(2,1)S(1)} %get-tuple-elem, ...), custom_call_target="tpu_custom_call" | custom-call | tf_op jit(solution)/shard_map/pallas_call | solution.py:1057

commit v3 on v2

--- a/solution.py
+++ b/solution.py
@@ -52,16 +52,17 @@
     other = 1 - core
     sib = (dp, mp + 1 - 2 * core)
     across = (dp, (mp + 2) % 4)
+    diagonal = (dp, (mp + 3 - 2 * core) % 4)
 
     bar = pltpu.get_barrier_semaphore()
-    for t in (sib, across):
+    for t in (sib, across, diagonal):
         pl.semaphore_signal(bar, inc=1, device_id=t, device_id_type=MESH)
     for d in range(1, n_dp):
         pl.semaphore_signal(bar, inc=1, device_id=((dp + d) % n_dp, mp), device_id_type=MESH)
 
     loads = []
     for i, (src, dst) in enumerate((
-        (ns.tokens, ns.tokens_v), (ns.wq, ns.wq_v), (ns.wk, ns.wk_v), (ns.wv, ns.wv_v), (ns.wo, ns.wo_v),
+        (ns.wo, ns.wo_all.at[mp]), (ns.tokens, ns.tokens_v), (ns.wq, ns.wq_v), (ns.wk, ns.wk_v), (ns.wv, ns.wv_v),
         (ns.wu, ns.wu_v), (ns.wd, ns.wd_v), (ns.og, ns.og_v),
     )):
         loads.append(pltpu.make_async_copy(src, dst, ns.in_sem.at[i]))
@@ -73,7 +74,7 @@
     )):
         n = x.shape[0]
         vecs[i : i + 1, 0:n] = x[...].reshape(1, n)
-    pl.semaphore_wait(bar, 1 + n_dp)
+    pl.semaphore_wait(bar, 2 + n_dp)
 
     sends = []
 
@@ -123,7 +124,7 @@
     def pair_copy(which, c):
         par = which % 2
         return remote(ns.part.at[par, c, pl.ds(pl.multiple_of(other * half, half), half)], ns.arecv.at[par, c],
-                      ns.a_s.at[par], ns.a_r.at[par, c], sib)
+                      ns.a_s.at[par, c], ns.a_r.at[par, c], sib)
 
     def cross_copy(which, c):
         par = which % 2
@@ -138,7 +139,7 @@
         if which >= 2:
             finish_send((0, which - 2, c))
         compute(c, put)
-        begin_send((0, which, c), (0, which % 2), pair_copy(which, c))
+        begin_send((0, which, c), (0, which % 2, c), pair_copy(which, c))
 
     def send_across(which, c):
         par = which % 2
@@ -159,10 +160,10 @@
     def halves(i, c):
         rows = pl.ds(pl.multiple_of(c * QB + core * half, half), half)
         x = (ns.hl, ns.res, ns.d2l, ns.d1l, ns.tg)[i]
-        return remote(x.at[rows], x.at[rows], ns.g_s.at[i], ns.g_r.at[G_SLOT[i], c], sib)
+        return remote(x.at[rows], x.at[rows], ns.g_s.at[i, c], ns.g_r.at[G_SLOT[i], c], sib)
 
     def to_sibling(i, c):
-        begin_send((2, i, c), (2, i), halves(i, c))
+        begin_send((2, i, c), (2, i, c), halves(i, c))
 
     TR = z.TR
 
@@ -209,10 +210,30 @@
             ctx = o if ctx is None else ctx + o
         ns.ctx[q0 : q0 + QB, :] = ctx.astype(BF16)
 
-    def attn_out(c, put):
-        x = ns.ctx[at_chunk(c), :]
+    def weight_copy(k):
+        if k == 2:
+            x = ns.wo_all.at[(mp + 2) % 4]
+        else:
+            x = ns.wo_all.at[mp]
+        return remote(x, x, ns.w_s.at[k], ns.w_r.at[k], (sib, across, sib)[k])
+
+    def context_copy(c, k):
+        mine = k == 1
+        rows = pl.ds(pl.multiple_of(c * QB + (core if mine else other) * half, half), half)
+        return remote(ns.ctx.at[rows], ns.ctx_all.at[c, mp], ns.cx_s.at[c, k], ns.cx_r.at[c, k], (sib, across, diagonal)[k])
+
+    def send_context(c):
+        for k in (1, 2, 0):
+            context_copy(c, k).start()
+            sends.append(context_copy(c, k))
+        ns.ctx_all[c, mp] = ns.ctx[row_ds(c, 0, half), :]
+
+    def attn_out(c):
         for w in columns(D):
-            put(w, nn(x, ns.wo_v[:, w]))
+            total = nn(ns.ctx_all[c, 0], ns.wo_all[0, :, w])
+            for k in range(1, 4):
+                total = total + nn(ns.ctx_all[c, k], ns.wo_all[k, :, w])
+            ns.dtok[:, w] = total
 
     def norm(v):
         mean = jnp.mean(v, axis=-1, keepdims=True)
@@ -223,7 +244,7 @@
     def first_norm(c):
         def body(rows, start):
             mine = row_ds(c, start, TR)
-            xh, rstd = norm(ns.tokens_v[mine].astype(F32) + y_total(0, c, rows) + vec(2))
+            xh, rstd = norm(ns.tokens_v[mine].astype(F32) + ns.dtok[rows] + vec(2))
             ns.xhat1[c, rows] = xh
             ns.rstd1[c, rows] = rstd
             h = xh * vec(3) + vec(4)
@@ -414,7 +435,7 @@
     def attend_back(c):
         r, b = c // n_qb, c % n_qb
         q0, k0 = c * QB, r * S + win(b)
-        cb = nt(ns.d1l[at_chunk(c), :], ns.wo_v[...]).astype(BF16)
+        cb = nt(ns.d1l[at_chunk(c), :], ns.wo_all[mp]).astype(BF16)
         qb = ns.q[q0 : q0 + QB, :]
         kb = ns.k[k0 : k0 + KW, :]
         vb = ns.v[k0 : k0 + KW, :]
@@ -781,19 +802,28 @@
     def come(i, c):
         once((i, c), halves(i, c).wait_recv)
 
+    load(0)
+    for k in (1, 0):
+        weight_copy(k).start()
+        sends.append(weight_copy(k))
     ns.pool[...] = jnp.zeros((PR, D), F32)
     ns.acc[...] = jnp.zeros(ns.acc.shape, F32)
 
     def run_project(r):
-        load(0, 1, 2, 3)
+        load(1, 2, 3, 4)
         project(r)
 
-    def run_out(c):
-        load(4)
-        send_part(0, c, attn_out)
+    def run_relay(_):
+        weight_copy(1).wait_recv()
+        weight_copy(2).start()
+        sends.append(weight_copy(2))
 
     def run_norm(c):
-        cross_copy(0, c).wait_recv()
+        for k in range(3):
+            context_copy(c, k).wait_recv()
+        for k in (0, 2):
+            once((8, k), weight_copy(k).wait_recv)
+        attn_out(c)
         first_norm(c)
         to_sibling(0, c)
 
@@ -811,13 +841,14 @@
         second_norm(c)
         to_sibling(1, c)
 
-    forward = (run_project, attend, run_out, functools.partial(send_across, 0), run_norm, run_up, run_down,
+    forward = (run_project, attend, send_context, run_relay, run_norm, run_up, run_down,
                functools.partial(send_across, 1), run_second)
     if NC == 4:
         plan = FORWARD
     else:
         plan = [r for r in range(R)]
-        for group in ((1, 2, 3), (4, 5, 6, 7), (8,)):
+        plan += [10 * k + c for c in range(NC) for k in (1, 2)] + [30]
+        for group in ((4, 5, 6, 7), (8,)):
             plan += [10 * k + c for c in range(NC) for k in group]
     for k in plan:
         forward[k // 10](k % 10)
@@ -928,8 +959,7 @@
 
 
 FORWARD = (
-    0, 10, 20, 1, 30, 11, 21, 12, 31, 22, 13, 32, 23, 33, 40, 50, 60, 41, 70, 51, 61, 42, 71, 52, 62, 43, 72,
-    53, 63, 73, 80, 81, 82, 83,
+    0, 10, 20, 1, 11, 21, 12, 22, 13, 23, 30, 40, 50, 60, 41, 70, 51, 61, 42, 71, 52, 62, 43, 72, 53, 63, 73, 80, 81, 82, 83,
 )
 JOBS = (
     (0, 0, 32), (1, 0, 32), (3, 0, 80), (0, 0, 32), (0, 0, 96), (1, 0, 64), (0, 0, 96), (0, 0, 96), (1, 0, 64),
@@ -1018,7 +1048,7 @@
     dma = pltpu.SemaphoreType.DMA
     scratch = dict(
         tokens_v=V((T, D), BF16), og_v=V((T, D), BF16), wq_v=V((L, D), BF16), wk_v=V((L, D), BF16),
-        wv_v=V((L, D), BF16), wo_v=V((L, D), BF16), wu_v=V((D, F), BF16), wd_v=V((F, D), BF16), vecs=V((9, D), F32),
+        wv_v=V((L, D), BF16), wo_all=V((4, L, D), BF16), ctx_all=V((NC, 4, half, L), BF16), wu_v=V((D, F), BF16), wd_v=V((F, D), BF16), vecs=V((9, D), F32),
         q=V((T, L), BF16), k=V((T, L), BF16), v=V((T, L), BF16), ctx=V((T, L), BF16),
         dq=V((T, L), BF16), dk=V((T, L), BF16), dv=V((T, L), BF16), dk_acc=V((S, L), F32), dv_acc=V((S, L), F32),
         probs=V((NC * heads, QB, KW), BF16),
@@ -1034,8 +1064,8 @@
         inc2=V((n_dp * 16, 128), BF16),
         vmine=V((8, D), F32), vsib=V((8, D), F32), vg=V((16, D // 2), BF16), vr=V((3, 16, D // 2), BF16),
         grad=V((3, D, D), BF16), rx=V((rx_rows, D), BF16),
-        in_sem=dma((8,)), a_s=dma((2,)), a_r=dma((2, NC)), y_s=dma((2, NC)), y_r=dma((2, NC)),
-        g_s=dma((5,)), g_r=dma((3, NC)), pool_sem=dma((4,)), p_s=dma((n_dp,)), p_r=dma((2, n_dp)),
+        in_sem=dma((8,)), w_s=dma((3,)), w_r=dma((3,)), cx_s=dma((NC, 3)), cx_r=dma((NC, 3)), a_s=dma((2, NC)), a_r=dma((2, NC)), y_s=dma((2, NC)), y_r=dma((2, NC)),
+        g_s=dma((5, NC)), g_r=dma((3, NC)), pool_sem=dma((4,)), p_s=dma((n_dp,)), p_r=dma((2, n_dp)),
         v_s=dma((2,)), v_r=dma((3,)), d_s=dma((n_slots, 2)), d_r=dma((n_jobs, 4)),
     )
     names = tuple(ins) + tuple(outs) + tuple(scratch)

time: 141 us -> 136 us (0.965)
  Pallas kernels: 140 us -> 135 us
    pallas_call x1, Pallas kernels: 135 us -> 129 us  [on_device(): pl.pallas_call(functools.partial(layer_kernel, z, names), out_shape=[V(*s...]
where the time goes in v3:
time: 136 us; the launch traced here: 135 us
  Pallas kernels  135 us (99%)
    pallas_call x1, Pallas kernels, on_device(): pl.pallas_call(functools.partial(layer_kernel, z, names), out_shape=[V(*s...  129 us
    pallas_call x1, Pallas kernels, on_device(): pl.pallas_call(functools.partial(unpack_kernel, z), out_shape=[jax.ShapeD...  5.09 us

profile of v3, /device:TPU:0, one launch (start us, length us, event | category | flops | bytes accessed | tf_op | source)
XLA Modules:
  0.0 135.4 jit_solution(14117018775250092958)
XLA Ops:
  0.7 129.4 %shard_map.331 = (bf16[1024,768]{1,0:T(8,128)(2,1)S(1)}, f32[1024,768]{1,0:T(8,128)S(1)}, bf16[3,768,768]{2,1,0:T(8,128)(2,1)S(1)}, bf16[16,384]{1,0:T(8,128)(2,1)S(1)}, f32[8,128]{1,0:T(8,128)S(1)}) custom-call(s32[2,7]{1,0:T(2,128)} %refs_0_.1, s32[12]{0:T(128)} %refs_1_.1, s32[16]{0:T(128)} %refs_2_.1, f32[192]{0:T(256)} %refs_3_.1, f32[192]{0:T(256)} %refs_4_.1, ...), custom_call_target="tpu_custom_call" | custom-call | tf_op jit(solution)/shard_map/pallas_call | solution.py:1072
  130.1 5.1 %shard_map.332 = (f32[768,768]{1,0:T(8,128)}, f32[768,768]{1,0:T(8,128)}, bf16[1024,768]{1,0:T(8,128)(2,1)}, f32[1024,768]{1,0:T(8,128)}, f32[192,768]{1,0:T(8,1...) custom-call(bf16[3,768,768]{2,1,0:T(8,128)(2,1)S(1)} %get-tuple-elem, ...), custom_call_target="tpu_custom_call" | custom-call | tf_op jit(solution)/shard_map/pallas_call | solution.py:1087

commit v4 on v3

--- a/solution.py
+++ b/solution.py
@@ -76,9 +76,8 @@
         vecs[i : i + 1, 0:n] = x[...].reshape(1, n)
     pl.semaphore_wait(bar, 2 + n_dp)
 
-    sends = []
-
     def remote(src, dst, ss, rs, to):
+        ss = ns.s_pool.at[0] if ss is None else ss
         return pltpu.make_async_remote_copy(
             src_ref=src, dst_ref=dst, send_sem=ss, recv_sem=rs, device_id=to, device_id_type=MESH
         )
@@ -105,30 +104,42 @@
     def only_head(x, h):
         return jnp.where(lane_head == h, x, jnp.zeros_like(x))
 
-    in_flight = {}
-    unsent = {}
+    users, taken = [None] * z.pool, [0]
+
+    def retire(i):
+        condition, copy, _ = users[i]
+        users[i] = None
+        if condition is None:
+            copy.wait_send()
+        else:
+            pl.when(condition)(copy.wait_send)
+
+    def take():
+        i = taken[0] % z.pool
+        taken[0] += 1
+        if users[i] is not None:
+            retire(i)
+        return i
+
+    def begin_send(build, key=None):
+        i = take()
+        copy = build(ns.s_pool.at[i])
+        copy.start()
+        users[i] = (None, copy, key)
 
     def finish_send(key):
-        if key in unsent:
-            sem, copy = unsent.pop(key)
-            copy.wait_send()
-            del in_flight[sem]
-
-    def begin_send(key, sem, copy):
-        if sem in in_flight:
-            finish_send(in_flight[sem])
-        in_flight[sem] = key
-        unsent[key] = (sem, copy)
-        copy.start()
-
-    def pair_copy(which, c):
+        for i, u in enumerate(users):
+            if u is not None and u[2] == key:
+                retire(i)
+
+    def pair_copy(which, c, ss=None):
         par = which % 2
         return remote(ns.part.at[par, c, pl.ds(pl.multiple_of(other * half, half), half)], ns.arecv.at[par, c],
-                      ns.a_s.at[par, c], ns.a_r.at[par, c], sib)
-
-    def cross_copy(which, c):
+                      ss, ns.a_r.at[par, c], sib)
+
+    def cross_copy(which, c, ss=None):
         par = which % 2
-        return remote(ns.ysend.at[par, c], ns.yrecv.at[par, c], ns.y_s.at[par, c], ns.y_r.at[par, c], across)
+        return remote(ns.ysend.at[par, c], ns.yrecv.at[par, c], ss, ns.y_r.at[par, c], across)
 
     def send_part(which, c, compute):
         part = ns.part.at[which % 2, c]
@@ -139,7 +150,7 @@
         if which >= 2:
             finish_send((0, which - 2, c))
         compute(c, put)
-        begin_send((0, which, c), (0, which % 2, c), pair_copy(which, c))
+        begin_send(functools.partial(pair_copy, which, c), (0, which, c))
 
     def send_across(which, c):
         par = which % 2
@@ -148,7 +159,7 @@
             finish_send((1, which - 2, c))
         own = pl.ds(pl.multiple_of(core * half, half), half)
         ns.ysend[par, c] = ns.part[par, c, own] + ns.arecv[par, c]
-        begin_send((1, which, c), (1, which % 2, c), cross_copy(which, c))
+        begin_send(functools.partial(cross_copy, which, c), (1, which, c))
 
     def y_total(which, c, rows):
         par = which % 2
@@ -157,13 +168,13 @@
     def at_chunk(c):
         return slice(c * QB, c * QB + QB)
 
-    def halves(i, c):
+    def halves(i, c, ss=None):
         rows = pl.ds(pl.multiple_of(c * QB + core * half, half), half)
         x = (ns.hl, ns.res, ns.d2l, ns.d1l, ns.tg)[i]
-        return remote(x.at[rows], x.at[rows], ns.g_s.at[i, c], ns.g_r.at[G_SLOT[i], c], sib)
+        return remote(x.at[rows], x.at[rows], ss, ns.g_r.at[G_SLOT[i], c], sib)
 
     def to_sibling(i, c):
-        begin_send((2, i, c), (2, i, c), halves(i, c))
+        begin_send(functools.partial(halves, i, c))
 
     TR = z.TR
 
@@ -210,22 +221,21 @@
             ctx = o if ctx is None else ctx + o
         ns.ctx[q0 : q0 + QB, :] = ctx.astype(BF16)
 
-    def weight_copy(k):
+    def weight_copy(k, ss=None):
         if k == 2:
             x = ns.wo_all.at[(mp + 2) % 4]
         else:
             x = ns.wo_all.at[mp]
-        return remote(x, x, ns.w_s.at[k], ns.w_r.at[k], (sib, across, sib)[k])
-
-    def context_copy(c, k):
+        return remote(x, x, ss, ns.w_r.at[k], (sib, across, sib)[k])
+
+    def context_copy(c, k, ss=None):
         mine = k == 1
         rows = pl.ds(pl.multiple_of(c * QB + (core if mine else other) * half, half), half)
-        return remote(ns.ctx.at[rows], ns.ctx_all.at[c, mp], ns.cx_s.at[c, k], ns.cx_r.at[c, k], (sib, across, diagonal)[k])
+        return remote(ns.ctx.at[rows], ns.ctx_all.at[c, mp], ss, ns.cx_r.at[c, k], (sib, across, diagonal)[k])
 
     def send_context(c):
         for k in (1, 2, 0):
-            context_copy(c, k).start()
-            sends.append(context_copy(c, k))
+            begin_send(functools.partial(context_copy, c, k))
         ns.ctx_all[c, mp] = ns.ctx[row_ds(c, 0, half), :]
 
     def attn_out(c):
@@ -319,29 +329,29 @@
     def unstack(x):
         return jnp.concatenate([x[c * PR : c * PR + PR] for c in range(CH)], axis=1)
 
-    def peers(src, dst, ssem, rsem):
-        cs = []
+    def peers(src, dst, rsem):
         mine = pl.ds(pl.multiple_of(dp * 16, 16), 16)
+
+        def copy(d, ss=None):
+            t = (dp + d) % n_dp
+            return remote(src.at[pl.ds(pl.multiple_of(t * 16, 16), 16)], dst.at[mine], ss, rsem.at[d], (t, mp))
+
         for d in range(1, n_dp):
-            t = (dp + d) % n_dp
-            c = remote(src.at[pl.ds(pl.multiple_of(t * 16, 16), 16)], dst.at[mine], ssem.at[d], rsem.at[d], (t, mp))
-            c.start()
-            cs.append(c)
+            begin_send(functools.partial(copy, d))
         dst[mine] = src[mine]
-        for c in cs:
-            c.wait()
+        for d in range(1, n_dp):
+            copy(d).wait_recv()
 
     def pairs():
-        c = remote(ns.pool, ns.pool_r, ns.pool_sem.at[0], ns.pool_sem.at[1], sib)
-        c.start()
+        begin_send(lambda ss: remote(ns.pool, ns.pool_r, ss, ns.pool_sem.at[0], sib))
         lens = [ns.lengths[s // 6, s % 6] for s in range(n_sent)]
         size = per_row(lens, 0, (PR, 1), 1).astype(F32)
         inv = 1.0 / size
         hot = slot_onehot(1)
-        c.wait()
+        remote(ns.pool, ns.pool_r, None, ns.pool_sem.at[0], sib).wait_recv()
         pooled = (ns.pool[...] + ns.pool_r[...]) * inv
         ns.outg[...] = nn(hot, stack(pooled).astype(BF16)).astype(BF16)
-        peers(ns.outg, ns.inc, ns.p_s, ns.p_r.at[0])
+        peers(ns.outg, ns.inc, ns.p_r.at[0])
         o = unstack(nn(place_onehot(1), ns.inc[...]))
         s = lax.rsqrt(jnp.sum(o * o, axis=-1, keepdims=True) + UNIT_EPS)
         u = o * s
@@ -367,7 +377,7 @@
         )
         do = s * (du - u * jnp.sum(u * du, axis=-1, keepdims=True))
         ns.outg2[...] = nn(place_onehot(0), stack(do).astype(BF16)).astype(BF16)
-        peers(ns.outg2, ns.inc2, ns.p_s, ns.p_r.at[1])
+        peers(ns.outg2, ns.inc2, ns.p_r.at[1])
         ns.dpool[...] = unstack(nn(slot_onehot(0), ns.inc2[...])) * inv
 
     def norm_back(dx, xh, rstd):
@@ -453,14 +463,14 @@
         ns.acc[7, :, :L] += fold(dq.astype(F32))
         at = slice(win(b), win(b) + KW)
         if b == 0:
-            ns.dk_acc[...] = jnp.zeros((S, L), F32)
-            ns.dv_acc[...] = jnp.zeros((S, L), F32)
-        ns.dk_acc[at, :] += dk
-        ns.dv_acc[at, :] += dv
+            ns.dk_acc[r] = jnp.zeros((S, L), F32)
+            ns.dv_acc[r] = jnp.zeros((S, L), F32)
+        ns.dk_acc[r, at, :] += dk
+        ns.dv_acc[r, at, :] += dv
         if b == n_qb - 1:
             rows = slice(r * S, r * S + S)
-            ns.dk[rows, :] = ns.dk_acc[...].astype(BF16)
-            dvr = ns.dv_acc[...].astype(BF16)
+            ns.dk[rows, :] = ns.dk_acc[r].astype(BF16)
+            dvr = ns.dv_acc[r].astype(BF16)
             ns.dv[rows, :] = dvr
             ns.acc[8, :, :L] += fold(dvr.astype(F32))
 
@@ -511,235 +521,120 @@
 
         lax.fori_loop(0, n // step, body, 0)
 
+    def step(condition, first, *builds):
+        def run():
+            at = [take() for _ in builds]
+
+            def body():
+                first()
+                for i, build in zip(at, builds):
+                    build(ns.s_pool.at[i]).start()
+
+            if condition is None:
+                body()
+            else:
+                pl.when(condition)(body)
+            for i, build in zip(at, builds):
+                users[i] = (condition, build(ns.s_pool.at[i]), None)
+
+        return run
+
+    def nothing():
+        pass
+
+    def copies(slot, *all_of):
+        return [
+            functools.partial(lambda src, dst, k, to, ss=None: remote(src, dst, ss, ns.d_r.at[slot, k], to), *one)
+            for one in all_of
+        ]
+
+    def got(*builds):
+        def first():
+            for build in builds:
+                build().wait_recv()
+
+        return first
+
+    def got_add(build, dst, row, at, n):
+        def first():
+            build().wait_recv()
+            add_into(dst, row, row, at, n)
+
+        return first
+
     def x_job(slot, j, r0, n):
         h = n // 2
         mine = pl.multiple_of(r0 + xi * h, 16)
         yours = pl.multiple_of(r0 + (1 - xi) * h, 16)
-        own, theirs = pl.ds(mine, h), pl.ds(yours, h)
-        s = lambda k: ns.d_s.at[z.slots[slot], k]
-        q = lambda k: ns.d_r.at[slot, k]
+        own, theirs = grad.at[j, pl.ds(mine, h)], grad.at[j, pl.ds(yours, h)]
+        done = gsum.at[j, pl.ds(mine, h)]
         b0 = z.rx_at[slot]
         buf = lambda k: ns.rx.at[pl.ds(b0 + k * h, h)]
-        x1 = remote(grad.at[j, theirs], buf(0), s(0), q(0), xp)
-        z1 = remote(grad.at[j, own], buf(1), s(0), q(1), zp)
-        z2 = remote(grad.at[j, own], buf(2), s(0), q(2), zq)
-        z3 = remote(gsum.at[j, own], gsum.at[j, own], s(1), q(1), zp)
-        x2 = remote(gsum.at[j, own], gsum.at[j, own], s(0), q(3), xp)
-
-        def s1o():
-            x1.wait()
-            add_into(grad, (j, mine), (j, mine), b0, h)
-            z1.start()
-
-        def s1i():
-            x1.wait()
-            add_into(grad, (j, mine), (j, mine), b0, h)
-
-        def s2():
-            z1.wait_recv()
-            add_into(grad, (j, mine), (j, mine), b0 + h, h)
-            z2.start()
-
-        def s3():
-            z2.wait()
-            add_into(gsum, (j, mine), (j, mine), b0 + 2 * h, h)
-            z3.start()
-            x2.start()
-
-        def s4():
-            z3.wait_recv()
-            z1.wait_send()
-            x2.start()
-
-        def end():
-            x2.wait_send()
-            pl.when(inner)(z3.wait_send)
-
-        steps = {0: x1.start, 1: when(outer, s1o), 8: when(inner, s1i), 2: when(inner, s2), 3: when(inner, s3),
-                 4: when(outer, s4), 5: x2.wait_recv}
-        return steps, end
-
-    def z_job(slot, j, r0, n):
-        h = n // 2
-        mine = pl.multiple_of(r0 + ii * h, 16)
-        yours = pl.multiple_of(r0 + (1 - ii) * h, 16)
-        own, theirs, whole = pl.ds(mine, h), pl.ds(yours, h), pl.ds(r0, n)
-        s = lambda k: ns.d_s.at[z.slots[slot], k]
-        q = lambda k: ns.d_r.at[slot, k]
-        b0 = z.rx_at[slot]
-        buf = lambda k: ns.rx.at[pl.ds(b0 + k * h, h)]
-        z1 = remote(grad.at[j, whole], ns.rx.at[pl.ds(b0 + n, n)], s(0), q(0), zp)
-        z2 = remote(grad.at[j, theirs], buf(0), s(0), q(1), zq)
-        x = remote(grad.at[j, own], buf(1), s(1), q(2), xp)
-        z2b = remote(gsum.at[j, own], gsum.at[j, own], s(0), q(3), zq)
-        z3a = remote(gsum.at[j, own], gsum.at[j, own], s(1), q(1), zp)
-        z3b = remote(gsum.at[j, theirs], gsum.at[j, theirs], s(0), q(2), zp)
-
-        def s1():
-            z1.wait_recv()
-            add_into(grad, (j, r0), (j, r0), b0 + n, n)
-            z2.start()
-
-        def s2():
-            z2.wait_recv()
-            add_into(grad, (j, mine), (j, mine), b0, h)
-            x.start()
-
-        def s3():
-            x.wait()
-            z2.wait_send()
-            add_into(gsum, (j, mine), (j, mine), b0 + h, h)
-            z2b.start()
-            z3a.start()
-
-        def s4():
-            z2b.wait()
-            z3b.start()
-
-        def s5():
-            z3a.wait_recv()
-            z3b.wait_recv()
-
-        def end():
-            pl.when(outer)(z1.wait_send)
-
-            @pl.when(inner)
-            def _():
-                z3a.wait_send()
-                z3b.wait_send()
-
-        steps = {0: when(outer, z1.start), 1: when(inner, s1), 2: when(inner, s2), 3: when(inner, s3),
-                 4: when(inner, s4), 5: when(outer, s5)}
-        return steps, end
-
-    def q_job(slot, j, r0, n):
+        x1, z1, z2, z3, x2 = copies(
+            slot, (theirs, buf(0), 0, xp), (own, buf(1), 1, zp), (own, buf(2), 2, zq), (done, done, 1, zp), (done, done, 3, xp)
+        )
+        return {
+            0: step(None, nothing, x1),
+            1: step(outer, got_add(x1, grad, (j, mine), b0, h), z1),
+            8: step(inner, got_add(x1, grad, (j, mine), b0, h)),
+            2: step(inner, got_add(z1, grad, (j, mine), b0 + h, h), z2),
+            3: step(inner, got_add(z2, gsum, (j, mine), b0 + 2 * h, h), z3, x2),
+            4: step(outer, got(z3), x2),
+            5: step(None, got(x2)),
+        }
+
+    def z_job(slot, j, r0, n, quarters=False):
         h, f = n // 2, n // 4
         mine = pl.multiple_of(r0 + ii * h, 16)
         yours = pl.multiple_of(r0 + (1 - ii) * h, 16)
-        own, theirs, whole = pl.ds(mine, h), pl.ds(yours, h), pl.ds(r0, n)
-        back_a = pl.ds(pl.multiple_of(mine + xi * f, 16), f)
-        back_b = pl.ds(pl.multiple_of(yours + xi * f, 16), f)
-        s = lambda k: ns.d_s.at[z.slots[slot], k]
-        q = lambda k: ns.d_r.at[slot, k]
+        own, theirs, whole = grad.at[j, pl.ds(mine, h)], grad.at[j, pl.ds(yours, h)], grad.at[j, pl.ds(r0, n)]
+        done, done_b = gsum.at[j, pl.ds(mine, h)], gsum.at[j, pl.ds(yours, h)]
+        back_a, back_b = done, done_b
+        if quarters:
+            back_a = gsum.at[j, pl.ds(pl.multiple_of(mine + xi * f, 16), f)]
+            back_b = gsum.at[j, pl.ds(pl.multiple_of(yours + xi * f, 16), f)]
         b0 = z.rx_at[slot]
         buf = lambda k: ns.rx.at[pl.ds(b0 + k * h, h)]
-        z1 = remote(grad.at[j, whole], ns.rx.at[pl.ds(b0 + n, n)], s(0), q(0), zp)
-        z2 = remote(grad.at[j, theirs], buf(0), s(0), q(1), zq)
-        x = remote(grad.at[j, own], buf(1), s(1), q(2), xp)
-        z2b = remote(gsum.at[j, own], gsum.at[j, own], s(0), q(3), zq)
-        z3a = remote(gsum.at[j, back_a], gsum.at[j, back_a], s(1), q(0), zp)
-        z3b = remote(gsum.at[j, back_b], gsum.at[j, back_b], s(0), q(1), zp)
-        xa = remote(gsum.at[j, back_a], gsum.at[j, back_a], s(0), q(2), xp)
-        xb = remote(gsum.at[j, back_b], gsum.at[j, back_b], s(1), q(3), xp)
-
-        def s1():
-            z1.wait_recv()
-            add_into(grad, (j, r0), (j, r0), b0 + n, n)
-            z2.start()
-
-        def s2():
-            z2.wait_recv()
-            add_into(grad, (j, mine), (j, mine), b0, h)
-            x.start()
-
-        def s3():
-            x.wait()
-            z2.wait_send()
-            add_into(gsum, (j, mine), (j, mine), b0 + h, h)
-            z2b.start()
-            z3a.start()
-
-        def s4():
-            z2b.wait()
-            z3b.start()
-
-        def s5():
-            z3a.wait_recv()
-            z1.wait_send()
-            xa.start()
-            z3b.wait_recv()
-            xb.start()
-
-        def s6():
-            xa.wait_recv()
-            xb.wait_recv()
-
-        def end():
-            @pl.when(outer)
-            def _():
-                xa.wait_send()
-                xb.wait_send()
-
-            @pl.when(inner)
-            def _():
-                z3a.wait_send()
-                z3b.wait_send()
-
-        steps = {0: when(outer, z1.start), 1: when(inner, s1), 2: when(inner, s2), 3: when(inner, s3),
-                 4: when(inner, s4), 5: when(outer, s5), 6: when(outer, s6)}
-        return steps, end
+        z1, z2, x, z2b, z3a, z3b, xa, xb = copies(
+            slot, (whole, ns.rx.at[pl.ds(b0 + n, n)], 0, zp), (theirs, buf(0), 1, zq), (own, buf(1), 2, xp),
+            (done, done, 3, zq), (back_a, back_a, 0, zp), (back_b, back_b, 1, zp), (back_a, back_a, 2, xp),
+            (back_b, back_b, 3, xp),
+        )
+        steps = {
+            0: step(outer, nothing, z1),
+            1: step(inner, got_add(z1, grad, (j, r0), b0 + n, n), z2),
+            2: step(inner, got_add(z2, grad, (j, mine), b0, h), x),
+            3: step(inner, got_add(x, gsum, (j, mine), b0 + h, h), z2b, z3a),
+            4: step(inner, got(z2b), z3b),
+        }
+        if quarters:
+            steps[5] = step(outer, got(z3a, z3b), xa, xb)
+            steps[6] = step(outer, got(xa, xb))
+        else:
+            steps[5] = step(outer, got(z3a, z3b))
+        return steps
 
     def u_job(slot, j, r0, n):
         near = pl.multiple_of(r0 + ii * n, 16)
         far = pl.multiple_of(r0 + (1 - ii) * n, 16)
-        near_d, far_d = pl.ds(near, n), pl.ds(far, n)
-        s = lambda k: ns.d_s.at[z.slots[slot], k]
-        q = lambda k: ns.d_r.at[slot, k]
+        near_g, far_g = grad.at[j, pl.ds(near, n)], grad.at[j, pl.ds(far, n)]
+        near_s, far_s = gsum.at[j, pl.ds(near, n)], gsum.at[j, pl.ds(far, n)]
         b0 = z.rx_at[slot]
         buf = lambda k: ns.rx.at[pl.ds(b0 + k * n, n)]
-        za = remote(grad.at[j, far_d], buf(0), s(0), q(0), zp)
-        ma = remote(grad.at[j, far_d], buf(1), s(0), q(1), zq)
-        zb = remote(grad.at[j, near_d], buf(0), s(1), q(0), zp)
-        xa = remote(grad.at[j, near_d], buf(1), s(1), q(1), xp)
-        zc = remote(gsum.at[j, near_d], gsum.at[j, near_d], s(0), q(2), zp)
-        mb = remote(gsum.at[j, near_d], gsum.at[j, near_d], s(0), q(3), zq)
-        zd = remote(gsum.at[j, far_d], gsum.at[j, far_d], s(1), q(2), zp)
-
-        def s1():
-            za.wait_recv()
-            add_into(grad, (j, far), (j, far), b0, n)
-            ma.start()
-
-        def s2():
-            ma.wait_recv()
-            add_into(grad, (j, near), (j, near), b0 + n, n)
-            zb.start()
-
-        def s3():
-            zb.wait_recv()
-            add_into(grad, (j, near), (j, near), b0, n)
-            xa.start()
-
-        def s4():
-            xa.wait_recv()
-            za.wait_send()
-            add_into(gsum, (j, near), (j, near), b0 + n, n)
-            zc.start()
-
-        def s5():
-            zc.wait_recv()
-            ma.wait_send()
-            mb.start()
-
-        def s6():
-            mb.wait_recv()
-            zb.wait_send()
-            zd.start()
-
-        def end():
-            @pl.when(outer)
-            def _():
-                xa.wait_send()
-                zc.wait_send()
-
-            @pl.when(inner)
-            def _():
-                mb.wait_send()
-                zd.wait_send()
-
-        steps = {0: when(outer, za.start), 1: when(inner, s1), 2: when(inner, s2), 3: when(outer, s3),
-                 4: when(outer, s4), 5: when(inner, s5), 6: when(inner, s6), 7: when(outer, zd.wait_recv)}
-        return steps, end
+        za, ma, zb, xa, zc, mb, zd = copies(
+            slot, (far_g, buf(0), 0, zp), (far_g, buf(1), 1, zq), (near_g, buf(0), 0, zp), (near_g, buf(1), 1, xp),
+            (near_s, near_s, 2, zp), (near_s, near_s, 3, zq), (far_s, far_s, 2, zp),
+        )
+        return {
+            0: step(outer, nothing, za),
+            1: step(inner, got_add(za, grad, (j, far), b0, n), ma),
+            2: step(inner, got_add(ma, grad, (j, near), b0 + n, n), zb),
+            3: step(outer, got_add(zb, grad, (j, near), b0, n), xa),
+            4: step(outer, got_add(xa, gsum, (j, near), b0 + n, n), zc),
+            5: step(inner, got(zc), mb),
+            6: step(inner, got(mb), zd),
+            7: step(outer, got(zd)),
+        }
 
     def vector_job():
         vg, vr = ns.vg, ns.vr
@@ -781,9 +676,8 @@
     tasks, ends_of = {}, {}
     if in_kernel:
         for i, (kind, j, r0, n) in enumerate(z.jobs):
-            steps, end = (x_job, z_job, q_job, u_job)[kind](i, j, r0, n)
-            tasks.update({JOB + i * 10 + k: f for k, f in steps.items()})
-            ends_of[i] = end
+            job = (x_job, z_job, functools.partial(z_job, quarters=True), u_job)[kind]
+            tasks.update({JOB + i * 10 + k: f for k, f in job(i, j, r0, n).items()})
         steps, end = vector_job()
         tasks.update({VECTOR + k: f for k, f in steps.items()})
         ends_of[-1] = end
@@ -804,8 +698,7 @@
 
     load(0)
     for k in (1, 0):
-        weight_copy(k).start()
-        sends.append(weight_copy(k))
+        begin_send(functools.partial(weight_copy, k))
     ns.pool[...] = jnp.zeros((PR, D), F32)
     ns.acc[...] = jnp.zeros(ns.acc.shape, F32)
 
@@ -815,8 +708,7 @@
 
     def run_relay(_):
         weight_copy(1).wait_recv()
-        weight_copy(2).start()
-        sends.append(weight_copy(2))
+        begin_send(functools.partial(weight_copy, 2))
 
     def run_norm(c):
         for k in range(3):
@@ -886,8 +778,8 @@
         for i in range(NC):
             come(1, i)
 
-    def vector_copy():
-        return remote(ns.vmine, ns.vsib, ns.pool_sem.at[2], ns.pool_sem.at[3], sib)
+    def vector_copy(ss=None):
+        return remote(ns.vmine, ns.vsib, ss, ns.pool_sem.at[1], sib)
 
     def run_vectors(_):
         for i in range(7):
@@ -895,10 +787,10 @@
         ns.vmine[7:8, :] = jnp.zeros((1, D), F32)
         ns.vmine[7:8, 0:L] = jnp.sum(ns.acc[7], axis=0, keepdims=True)[:, :L]
         ns.vmine[7:8, 256 : 256 + L] = jnp.sum(ns.acc[8], axis=0, keepdims=True)[:, :L]
-        vector_copy().start()
+        begin_send(vector_copy)
 
     def run_vectors_sum(_):
-        vector_copy().wait()
+        vector_copy().wait_recv()
         v = ns.vmine[...] + jnp.where(iota((8, D), 0) < 6, ns.vsib[...], 0.0)
         ns.vg[...] = jnp.concatenate([v[:, : D // 2], v[:, D // 2 :]], axis=0).astype(BF16)
 
@@ -910,8 +802,6 @@
     )
     for k in z.order:
         if k in tasks:
-            if k in z.free_before:
-                ends_of.pop(z.free_before[k])()
             tasks[k]()
         elif k < VECTOR:
             backward[k // 10](k % 10)
@@ -920,10 +810,9 @@
     if not in_kernel:
         gsum[...] = grad[...]
         ns.vt[...] = ns.vg[...]
-    for key in list(unsent):
-        finish_send(key)
-    for c in sends:
-        c.wait_send()
+    for i, u in enumerate(users):
+        if u is not None:
+            retire(i)
 
 
 def unpack_kernel(z, g, res_i, tg_i, vec, loss_i, gd, gu, res, tg, gq, gk, gv, go, *more):
@@ -962,45 +851,33 @@
     0, 10, 20, 1, 11, 21, 12, 22, 13, 23, 30, 40, 50, 60, 41, 70, 51, 61, 42, 71, 52, 62, 43, 72, 53, 63, 73, 80, 81, 82, 83,
 )
 JOBS = (
-    (0, 0, 32), (1, 0, 32), (3, 0, 80), (0, 0, 32), (0, 0, 96), (1, 0, 64), (0, 0, 96), (0, 0, 96), (1, 0, 64),
-    (0, 0, 96), (3, 1, 80), (0, 1, 96), (1, 1, 96), (0, 1, 96), (0, 1, 96), (0, 1, 96), (1, 1, 64), (0, 1, 64),
-    (0, 2, 96), (1, 2, 64), (0, 2, 96), (1, 2, 64), (0, 2, 96), (1, 2, 64), (0, 2, 96), (1, 2, 64), (0, 2, 64),
-    (1, 2, 64),
+    (3, 0, 48), (0, 0, 128), (3, 0, 32), (0, 0, 96), (0, 0, 96), (0, 0, 96), (2, 0, 64), (1, 0, 32),
+    (0, 0, 32), (0, 0, 32), (0, 0, 32), (0, 1, 96), (3, 1, 32), (0, 1, 32), (0, 1, 96), (1, 1, 96), (0, 1, 32),
+    (0, 1, 128), (1, 1, 32), (0, 1, 32), (0, 1, 32), (0, 1, 32), (2, 1, 64), (0, 1, 32), (0, 2, 96),
+    (3, 2, 32), (0, 2, 96), (3, 2, 32), (0, 2, 96), (0, 2, 96), (0, 2, 64), (2, 2, 128), (0, 2, 64),
 )
 VECTOR, JOB = 200, 1000
 ORDER = (
-    0, 1, 2, 3, 21, 10, 1010, 1000, 11, 1040, 1030, 1020, 12, 1070, 22, 1050, 31, 23, 20, 1080, 1060, 30, 1048,
-    1011, 50, 51, 1110, 1021, 41, 1012, 1100, 1051, 40, 1013, 1130, 32, 1078, 1120, 52, 1081, 1068, 1041, 1071,
-    42, 1052, 1022, 61, 1101, 1170, 1160, 1140, 1001, 33, 1053, 1121, 1082, 1061, 1178, 1014, 1141, 1150, 60,
-    1102, 1042, 43, 1031, 70, 1072, 1090, 1138, 1054, 71, 1122, 1023, 1083, 1161, 1148, 1008, 1043, 1073, 1131,
-    1062, 62, 1151, 1002, 1103, 80, 1091, 63, 1142, 1098, 1158, 1123, 1084, 72, 1162, 1132, 1063, 1118, 1024,
-    73, 140, 1003, 90, 1143, 1152, 100, 82, 1190, 1104, 1092, 1111, 1124, 1163, 81, 1133, 150, 92, 1180, 1210,
-    1220, 1025, 1240, 1004, 1074, 1144, 1191, 91, 1250, 1153, 83, 1093, 1015, 1038, 1105, 1055, 1026, 1164,
-    130, 1171, 1145, 1032, 1260, 1211, 93, 1192, 200, 1112, 1154, 1181, 1064, 1200, 1106, 1075, 1033, 1230,
-    1188, 1228, 110, 1270, 1085, 1251, 1134, 201, 1172, 1212, 1193, 1221, 1034, 1113, 1261, 120, 1044, 1182,
-    1231, 112, 1201, 1173, 1213, 1174, 111, 1114, 1252, 1005, 1094, 121, 1271, 1194, 202, 1248, 1107, 1183,
-    1268, 1035, 1241, 1222, 1184, 1095, 1224, 204, 1065, 1214, 1027, 1215, 1232, 1125, 1253, 1208, 1202, 203,
-    1135, 1204, 113, 1272, 1264, 1262, 1244, 1223, 1185, 1242, 1233, 1155, 1115, 1175, 1255, 1203, 1045, 1263,
-    123, 122, 1243, 1225, 1165, 1205, 1273, 1265, 1195, 1254, 1245, 1234, 1235, 1274, 1275,
+    0, 1, 2, 3, 21, 10, 1000, 1010, 11, 1030, 31, 1020, 22, 12, 1060, 41, 1090, 32, 1050, 23, 1001, 20, 1011,
+    50, 1021, 1120, 1080, 30, 1110, 51, 40, 1100, 1160, 52, 1210, 1031, 1170, 1061, 42, 1220, 1002, 1200, 1018,
+    33, 1121, 1130, 1091, 1098, 1051, 1062, 1101, 1012, 1118, 1038, 1022, 1140, 1032, 60, 1190, 1230, 1092,
+    1221, 61, 1058, 1013, 1208, 1063, 1023, 1052, 43, 1108, 1040, 1218, 1211, 1171, 1150, 1168, 70, 1178, 1033,
+    1122, 1003, 1212, 1093, 1161, 1102, 62, 71, 1172, 1088, 1222, 1238, 1201, 1014, 1111, 1064, 72, 1213, 130,
+    1053, 1024, 1151, 1202, 1231, 1162, 1034, 80, 1112, 1103, 1180, 1148, 1223, 63, 1141, 1048, 1094, 1065,
+    1152, 1173, 1025, 1123, 1232, 73, 1113, 1203, 1054, 1181, 1041, 1142, 1138, 100, 1290, 1224, 1153, 1042,
+    1250, 140, 83, 1320, 1124, 1026, 1182, 1260, 90, 1143, 1251, 1271, 1280, 1154, 1104, 81, 1270, 91, 150,
+    1298, 1292, 1191, 201, 1328, 200, 1240, 1174, 1291, 1163, 1131, 93, 1198, 1310, 1125, 1252, 1261, 1144,
+    1233, 1132, 1183, 1204, 1268, 1114, 1300, 1081, 1253, 1192, 1272, 1321, 202, 1293, 1281, 1311, 1115, 1273,
+    1164, 1035, 1015, 1225, 1043, 1234, 1070, 1241, 1082, 1262, 1294, 1288, 1301, 1184, 1322, 1127, 1126, 82,
+    1254, 1312, 1133, 1134, 1193, 1194, 1248, 1214, 1027, 111, 1044, 1084, 1274, 203, 1308, 1083, 110, 1282,
+    1155, 1263, 1066, 1071, 1055, 1323, 1165, 1004, 1242, 1264, 1185, 1302, 92, 1283, 1324, 1072, 1313, 1295,
+    1243, 1255, 1275, 1284, 121, 1244, 1304, 1135, 1215, 1095, 1315, 1303, 1314, 1005, 113, 1256, 204, 1276,
+    1085, 112, 1073, 1045, 1006, 1325, 1007, 1145, 122, 1277, 1245, 1205, 1105, 120, 123, 1235, 1285, 1305,
+    1195, 1265, 1257, 1175, 1316, 1226, 1074, 1075,
 )
 G_SLOT = (0, 1, 0, 0, 2)
 VMEM1 = 54 * 2**20
-
-
-def send_slots(order, n_jobs):
-    steps = [(n, k, (k - JOB) // 10) for n, k in enumerate(order) if k >= JOB]
-    last = {i: n for n, _, i in steps}
-    slots, free_before, done, used = {}, {}, [], 0
-    for n, k, i in steps:
-        if i not in slots:
-            if done:
-                old = done.pop(0)
-                slots[i], free_before[k] = slots[old], old
-            else:
-                slots[i], used = used, used + 1
-        if last[i] == n:
-            done.append(i)
-    return slots, free_before, used
+POOL = 48
 
 
 def default_order(chunks):
@@ -1030,11 +907,10 @@
         at[j] += 2 * n if kind == 3 else n
         rx_rows += n // 2 * 3 if kind == 0 else 2 * n
     n_jobs = len(jobs)
-    slots, free_before, n_slots = send_slots(ORDER, n_jobs)
     order = ORDER if NC == 4 else default_order(NC)
     in_kernel = n_dp == 8 and at == [D, D, D] and NC == 4
     z = types.SimpleNamespace(n_dp=n_dp, R=R, S=S, D=D, L=L, F=F, heads=heads, in_kernel=in_kernel, QB=QB, KW=KW, TR=32,
-                              unroll=4, jobs=jobs, rx_at=rx_at, order=order, slots=slots, free_before=free_before)
+                              unroll=4, jobs=jobs, rx_at=rx_at, order=order, pool=POOL)
     ins = dict(lengths=lengths, send_slot=send_slot, recv_place=recv_place, b_query=b_query, b_value=b_value,
                output_bias=output_bias, first_norm_gain=first_norm_gain, first_norm_bias=first_norm_bias, b_up=b_up,
                down_bias=down_bias, second_norm_gain=second_norm_gain, second_norm_bias=second_norm_bias,
@@ -1050,7 +926,7 @@
         tokens_v=V((T, D), BF16), og_v=V((T, D), BF16), wq_v=V((L, D), BF16), wk_v=V((L, D), BF16),
         wv_v=V((L, D), BF16), wo_all=V((4, L, D), BF16), ctx_all=V((NC, 4, half, L), BF16), wu_v=V((D, F), BF16), wd_v=V((F, D), BF16), vecs=V((9, D), F32),
         q=V((T, L), BF16), k=V((T, L), BF16), v=V((T, L), BF16), ctx=V((T, L), BF16),
-        dq=V((T, L), BF16), dk=V((T, L), BF16), dv=V((T, L), BF16), dk_acc=V((S, L), F32), dv_acc=V((S, L), F32),
+        dq=V((T, L), BF16), dk=V((T, L), BF16), dv=V((T, L), BF16), dk_acc=V((R, S, L), F32), dv_acc=V((R, S, L), F32),
         probs=V((NC * heads, QB, KW), BF16),
         xhat1=V((NC, half, D), F32), xhat2=V((NC, half, D), F32), hid=V((NC, half, D), F32), d2=V((NC, half, D), F32),
         d1=V((NC, half, D), F32), rstd1=V((NC, half, 1), F32), rstd2=V((NC, half, 1), F32),
@@ -1064,9 +940,9 @@
         inc2=V((n_dp * 16, 128), BF16),
         vmine=V((8, D), F32), vsib=V((8, D), F32), vg=V((16, D // 2), BF16), vr=V((3, 16, D // 2), BF16),
         grad=V((3, D, D), BF16), rx=V((rx_rows, D), BF16),
-        in_sem=dma((8,)), w_s=dma((3,)), w_r=dma((3,)), cx_s=dma((NC, 3)), cx_r=dma((NC, 3)), a_s=dma((2, NC)), a_r=dma((2, NC)), y_s=dma((2, NC)), y_r=dma((2, NC)),
-        g_s=dma((5, NC)), g_r=dma((3, NC)), pool_sem=dma((4,)), p_s=dma((n_dp,)), p_r=dma((2, n_dp)),
-        v_s=dma((2,)), v_r=dma((3,)), d_s=dma((n_slots, 2)), d_r=dma((n_jobs, 4)),
+        in_sem=dma((8,)), w_r=dma((3,)), cx_r=dma((NC, 3)), a_r=dma((2, NC)), y_r=dma((2, NC)),
+        g_r=dma((3, NC)), pool_sem=dma((2,)), s_pool=dma((POOL,)), p_r=dma((2, n_dp)),
+        v_s=dma((2,)), v_r=dma((3,)), d_r=dma((n_jobs, 4)),
     )
     names = tuple(ins) + tuple(outs) + tuple(scratch)
     res, tg, grads, vec, loss = pl.pallas_call(

time: 136 us -> 129 us (0.949)
  Pallas kernels: 135 us -> 128 us
    pallas_call x1, Pallas kernels: 129 us -> 123 us  [on_device(): pl.pallas_call(functools.partial(layer_kernel, z, names), out_shape=[V(*s...]
where the time goes in v4:
time: 129 us
  Pallas kernels  128 us (99%)
    pallas_call x1, Pallas kernels, on_device(): pl.pallas_call(functools.partial(layer_kernel, z, names), out_shape=[V(*s...  123 us
    pallas_call x1, Pallas kernels, on_device(): pl.pallas_call(functools.partial(unpack_kernel, z), out_shape=[jax.ShapeD...  5.09 us

profile of v4, /device:TPU:0, one launch (start us, length us, event | category | flops | bytes accessed | tf_op | source)
XLA Modules:
  0.0 129.1 jit_solution(1505241947299674073)
XLA Ops:
  0.7 123.2 %shard_map.331 = (bf16[1024,768]{1,0:T(8,128)(2,1)S(1)}, f32[1024,768]{1,0:T(8,128)S(1)}, bf16[3,768,768]{2,1,0:T(8,128)(2,1)S(1)}, bf16[16,384]{1,0:T(8,128)(2,1)S(1)}, f32[8,128]{1,0:T(8,128)S(1)}) custom-call(s32[2,7]{1,0:T(2,128)} %refs_0_.1, s32[12]{0:T(128)} %refs_1_.1, s32[16]{0:T(128)} %refs_2_.1, f32[192]{0:T(256)} %refs_3_.1, f32[192]{0:T(256)} %refs_4_.1, ...), custom_call_target="tpu_custom_call" | custom-call | tf_op jit(solution)/shard_map/pallas_call | solution.py:948
  123.9 5.1 %shard_map.332 = (f32[768,768]{1,0:T(8,128)}, f32[768,768]{1,0:T(8,128)}, bf16[1024,768]{1,0:T(8,128)(2,1)}, f32[1024,768]{1,0:T(8,128)}, f32[192,768]{1,0:T(8,1...) custom-call(bf16[3,768,768]{2,1,0:T(8,128)(2,1)S(1)} %get-tuple-elem, ...), custom_call_target="tpu_custom_call" | custom-call | tf_op jit(solution)/shard_map/pallas_call | solution.py:963
